TPU v7x, 128 devices: a whole 4x4x4 slice. The times are simulated.
128 devices in a mesh: gx: 8 (over x, core), gy: 16 (over y, z).
Axes of the slice: x: 4, y: 4, z: 4, core: 2. Of those that a mesh axis runs over, the one named last changes fastest.
Arguments:
- concentration: float32 [768, 5, 32768], P(('gx', 'gy')), may hold values from 0.05 to 3
- neighbours: int32 [768, 6], P(('gx', 'gy')), may hold values from -1 to 767, as said below
- source_slot: int32 [768], P(('gx', 'gy')), may hold values from -1 to 767, as said below
- mobility: float32 [5], replicated, may hold values from 0.3 to 2
- fermi_gain: float32 [5], replicated, may hold values from 0.3 to 3
- rates: float32 [5], replicated, may hold values from 0.05 to 0.5
Outputs:
- moved: float32 [768, 5, 32768], P(('gx', 'gy'))
Inputs may be any that keep to these rules, and one draw needn't show every extreme that they name: neighbours: each entry is -1 or a slot on the same device or on a device next to it along gx or along gy (same index on the other axis); every slot that source_slot names has neighbours that name only such slots that source_slot names too or -1. source_slot: each entry is -1 or a slot on the same device or on a device next to it along gx or along gy; no slot is named twice; only slots below 2 of a device are other than -1; at most 1 slots of one device name slots of one other device, and some device names exactly 1 of a neighbour's.
All inputs are finite; a program needn't handle non-finite values.
Results may differ from a plain program's by a relative error of at most 0.0003.
Values sent between devices are 32-bit elements; how exact they have to be, the bound alone decides.
A program may use at most 192 MiB of HBM per device.

v0:
```python
import functools

import jax
import jax.numpy as jnp
from jax import lax
from jax.experimental import pallas as pl
from jax.experimental.pallas import tpu as pltpu
from jax.sharding import PartitionSpec as P

B = 32
SPECIES = 5
SWEEPS = 3
KEEP = 2
MOVE = 1
CAP = 6
ROWS = 256
ROOM = 6
MESH = pl.DeviceIdType.MESH

NEAR = ((-1, 0), (1, 0), (0, -1), (0, 1))
FAR = ((-2, 0), (2, 0), (0, -2), (0, 2), (-1, -1), (-1, 1), (1, -1), (1, 1))
AROUND = NEAR + FAR
ORDER = (2, 3, 0, 1)
PLACE = {(0, 0): 0, **{step: i + 1 for i, step in enumerate(AROUND)}}


def iota(shape, dim):
    return lax.broadcasted_iota(jnp.int32, shape, dim)


def exchange_kernel(
    nx, ny,
    conc, nbr_s, src_s, nbr_v, src_v,
    landp, landg, ghost_out, flag_out,
    raw, dense, own_faces, meta, table, table_s, sendp, sendf, landf, sendg, flags,
    in_sem, meta_ss, meta_rs, tab_sem, p_ss, p_rs, f_ss, f_rs, g_ss, g_rs, fl_ss, fl_rs,
):
    gx, gy = lax.axis_index("gx"), lax.axis_index("gy")
    me = gx * ny + gy

    def inside(step):
        x, y = gx + step[0], gy + step[1]
        return (x >= 0) & (x < nx) & (y >= 0) & (y < ny)

    def at(step):
        return (gx + step[0], gy + step[1])

    load = pltpu.make_async_copy(conc, raw, in_sem)
    load.start()

    row, col = gy // 4, gy % 4
    ring = (
        [((gx + k) % nx, gy) for k in range(1, nx)],
        [(gx, ((row + k) % 4) * 4 + col) for k in range(1, 4)],
        [(gx, row * 4 + (col + k) % 4) for k in range(1, 4)],
    )

    meta[...] = jnp.full(meta.shape, -1, jnp.int32)
    meta[0, 0:CAP, 0:6] = nbr_v[...]
    meta[0, CAP:CAP + 1, 0:CAP] = src_v[...]

    barrier = pltpu.get_barrier_semaphore()
    expected = nx - 1 + 6
    for step in AROUND:
        there = inside(step)
        expected = expected + there.astype(jnp.int32)

        @pl.when(there)
        def _():
            pl.semaphore_signal(barrier, inc=1, device_id=at(step), device_id_type=MESH)
    for group in ring:
        for target in group:
            pl.semaphore_signal(barrier, inc=1, device_id=target, device_id_type=MESH)
    load.wait()

    def spread_out(k, carry):
        s, x = k // B, k % B
        planes = raw[s, :, pl.ds(pl.multiple_of(x * 1024, 1024), 1024)].reshape(CAP, 8, 128)
        for q in range(CAP):
            dense[q, s, pl.ds(pl.multiple_of(x * 8, 8), 8), :] = planes[q]
        return carry

    lax.fori_loop(0, SPECIES * B, spread_out, 0)

    pl.semaphore_wait(barrier, expected)

    def opposite(i):
        return AROUND.index((-AROUND[i][0], -AROUND[i][1]))

    def meta_send(i):
        return pltpu.make_async_remote_copy(
            src_ref=meta.at[0], dst_ref=meta.at[1 + opposite(i)],
            send_sem=meta_ss.at[i], recv_sem=meta_rs.at[opposite(i)], device_id=at(AROUND[i]), device_id_type=MESH)

    for i, step in enumerate(AROUND):
        @pl.when(inside(step))
        def _():
            meta_send(i).start()

    lane8 = iota((8, 128), 1)

    def faces(k, carry):
        q, s = k // SPECIES, k % SPECIES
        own_faces[q * 6 + 0, s] = dense[q, s, 0:8, :]
        own_faces[q * 6 + 1, s] = dense[q, s, ROWS - 8:ROWS, :]
        low = jnp.zeros((8, 128), jnp.float32)
        high = jnp.zeros((8, 128), jnp.float32)
        for b in range(4):
            first = dense[q, s, pl.ds(64 * b, 8, stride=8), :]
            final = dense[q, s, pl.ds(64 * b + 7, 8, stride=8), :]
            here = lane8 // 32 == b
            low = jnp.where(here, pltpu.roll(first, 32 * b, 1) if b else first, low)
            high = jnp.where(here, pltpu.roll(final, 32 * (b + 1), 1) if b < 3 else final, high)
        own_faces[q * 6 + 2, s] = low
        own_faces[q * 6 + 3, s] = high
        low = jnp.zeros((8, 128), jnp.float32)
        high = jnp.zeros((8, 128), jnp.float32)
        for x in range(B):
            turned = pltpu.roll(dense[q, s, 8 * x:8 * x + 8, :], x + 1, 1)
            high = jnp.where(lane8 % 32 == x, turned, high)
            low = jnp.where(lane8 % 32 == (x + 1) % 32, turned, low)
        own_faces[q * 6 + 4, s] = pltpu.roll(low, 127, 1)
        own_faces[q * 6 + 5, s] = pltpu.roll(high, 96, 1)
        return carry

    lax.fori_loop(0, CAP * SPECIES, faces, 0)

    for i, step in enumerate(AROUND):
        @pl.when(inside(step))
        def _():
            meta_send(i).wait_send()
            pltpu.make_async_remote_copy(
                src_ref=meta.at[0], dst_ref=meta.at[1 + i], send_sem=meta_ss.at[i], recv_sem=meta_rs.at[i],
                device_id=at(step), device_id_type=MESH).wait_recv()

    def device(step):
        return me + step[0] * ny + step[1]

    def sources(step):
        return meta[PLACE[step], CAP:CAP + 1, :]

    taken = []
    for d, step in enumerate(NEAR):
        rel = sources(step) - me * CAP
        slot = jnp.max(jnp.where((rel >= 0) & (rel < CAP), rel, -1))
        taken.append(slot)
    safe = [jnp.maximum(slot, 0) for slot in taken]

    def patch_send(d, s):
        return pltpu.make_async_remote_copy(
            src_ref=sendp.at[d, s], dst_ref=landp.at[d ^ 1, s], send_sem=p_ss.at[d, s], recv_sem=p_rs.at[d ^ 1, s],
            device_id=at(NEAR[d]), device_id_type=MESH)

    def patch_wait(d, s):
        return pltpu.make_async_remote_copy(
            src_ref=sendp.at[d, s], dst_ref=landp.at[d, s], send_sem=p_ss.at[d, s], recv_sem=p_rs.at[d, s],
            device_id=at(NEAR[d]), device_id_type=MESH)

    def patches(some):
        for d in ORDER:
            @pl.when(inside(NEAR[d]))
            def _():
                for s in some:
                    def stage(r, carry):
                        part = pl.ds(pl.multiple_of(r * 64, 64), 64)
                        sendp[d, s, part, :] = dense[safe[d], s, part, :]
                        return carry
                    lax.fori_loop(0, 4, stage, 0)
                    patch_send(d, s).start()

    patches((0,))

    def face_send(d):
        return pltpu.make_async_remote_copy(
            src_ref=sendf.at[d], dst_ref=landf.at[d ^ 1], send_sem=f_ss.at[d], recv_sem=f_rs.at[d ^ 1],
            device_id=at(NEAR[d]), device_id_type=MESH)

    def face_wait(d):
        return pltpu.make_async_remote_copy(
            src_ref=sendf.at[d], dst_ref=landf.at[d], send_sem=f_ss.at[d], recv_sem=f_rs.at[d],
            device_id=at(NEAR[d]), device_id_type=MESH)

    def ghost_send(d):
        return pltpu.make_async_remote_copy(
            src_ref=sendg.at[d], dst_ref=landg.at[d ^ 1], send_sem=g_ss.at[d], recv_sem=g_rs.at[d ^ 1],
            device_id=at(NEAR[d]), device_id_type=MESH)

    def ghost_wait(d):
        return pltpu.make_async_remote_copy(
            src_ref=sendg.at[d], dst_ref=landg.at[d], send_sem=g_ss.at[d], recv_sem=g_rs.at[d],
            device_id=at(NEAR[d]), device_id_type=MESH)

    side = iota((8, 128), 1)
    far_side = side + 1 - 2 * (side % 2)
    slot_row = iota((8, 128), 0)
    lane1 = iota((1, 128), 1)

    def named(step):
        owner = device(step)
        hit = jnp.zeros((8, 128), jnp.bool_)
        for extra in ((0, 0),) + NEAR:
            hit = hit | (sources((step[0] + extra[0], step[1] + extra[1])) == owner * CAP + slot_row)
        return jnp.max(hit.astype(jnp.int32), axis=1, keepdims=True) > 0

    def wanted(step, of, names):
        rel = meta[PLACE[step]] - device(of) * CAP
        good = names & (rel >= 0) & (rel < CAP) & (slot_row < CAP) & (side < 6)
        code = jnp.where(good, rel * 6 + far_side, 127)
        hit = jnp.zeros((8, 128), jnp.bool_)
        for f in range(6):
            hit = hit | (code[:, f:f + 1] == side)
        mask = jnp.max(hit.astype(jnp.int32), axis=0, keepdims=True)
        mask = jnp.where(lane1 < 36, mask, 0)
        total = mask
        for k in (1, 2, 4, 8, 16, 32):
            total = total + jnp.where(lane1 >= k, pltpu.roll(total, k, 1), 0)
        return mask, total - mask

    mine = named((0, 0))
    over = jnp.zeros((8, 128), jnp.int32)
    for d, step in enumerate(NEAR):
        mask, rank = wanted(step, (0, 0), named(step))
        over = jnp.maximum(over, jnp.where((mask > 0) & (rank >= ROOM), 1, 0))
        chosen = jnp.where((mask > 0) & (rank == slot_row), side, 0)
        table[d] = jnp.broadcast_to(jnp.max(chosen, axis=1, keepdims=True), (8, 128))
        _, rank = wanted((0, 0), step, mine)
        table[4, d:d + 1, :] = rank
    over = jnp.broadcast_to(jnp.max(jnp.max(over, axis=1, keepdims=True), axis=0, keepdims=True), (8, 128))
    flags[0] = over
    to_scalars = pltpu.make_async_copy(table, table_s, tab_sem)
    to_scalars.start()

    to_scalars.wait()
    for d in ORDER:
        @pl.when(inside(NEAR[d]))
        def _():
            def stage(p, carry):
                sendf[d, p] = own_faces[table_s[d, p, 0]]
                return carry
            lax.fori_loop(0, ROOM, stage, 0)
            face_send(d).start()

    def flag_copy(base, k, target, held):
        return pltpu.make_async_remote_copy(
            src_ref=flags.at[held], dst_ref=flags.at[base + k], send_sem=fl_ss.at[base + k],
            recv_sem=fl_rs.at[base + k], device_id=target, device_id_type=MESH)

    bases = (3, 3 + nx - 1, 3 + nx - 1 + 3)
    for k, target in enumerate(ring[0]):
        flag_copy(bases[0], k, target, 0).start()
    patches((1, 2, 3, 4))

    for d, step in enumerate(NEAR):
        @pl.when(inside(step))
        def _():
            face_wait(d).wait_recv()

    def ghost_place(slot, f):
        nb = nbr_s[slot, f]
        rel = nb - me * CAP
        here = (rel >= 0) & (rel < CAP)
        opposite_f = f + 1 - 2 * (f % 2)
        own = jnp.where(here, rel * 6 + opposite_f, slot * 6 + f)
        own = jnp.where((nb < 0) | here, own, 0)
        away = jnp.int32(-1)
        for d, step in enumerate(NEAR):
            rel = nb - device(step) * CAP
            there = (nb >= 0) & (rel >= 0) & (rel < CAP)
            code = jnp.where(there, rel * 6 + opposite_f, 0)
            away = jnp.where(there, d * ROOM + jnp.minimum(table_s[4, d, code], ROOM - 1), away)
        return own, away

    def ghost_value(slot, f):
        own, away = ghost_place(slot, f)
        other = jnp.maximum(away, 0)
        return jnp.where(away >= 0, landf[other // ROOM, other % ROOM], own_faces[own])

    for d, step in enumerate(NEAR):
        @pl.when(inside(step))
        def _():
            def stage(f, carry):
                sendg[d, f] = ghost_value(safe[d], f)
                return carry
            lax.fori_loop(0, 6, stage, 0)
            ghost_send(d).start()

    def flag_round(n, held, following):
        for k, target in enumerate(ring[n]):
            copy = flag_copy(bases[n], k, target, held)
            copy.wait()
        total = flags[held]
        for k in range(len(ring[n])):
            total = jnp.maximum(total, flags[bases[n] + k])
        if following is None:
            flag_out[...] = total
        else:
            flags[following] = total
            for k, target in enumerate(ring[n + 1]):
                flag_copy(bases[n + 1], k, target, following).start()

    flag_round(0, 0, 1)

    for t in range(KEEP):
        rel = src_s[0, t] - me * CAP
        slot = jnp.where((rel >= 0) & (rel < CAP), rel, 0)

        def layer(f, carry):
            ghost_out[t, f] = ghost_value(slot, f)
            return carry
        lax.fori_loop(0, 6, layer, 0)

    flag_round(1, 1, 2)
    flag_round(2, 2, None)

    for d, step in enumerate(NEAR):
        @pl.when(inside(step))
        def _():
            face_send(d).wait_send()
            ghost_send(d).wait_send()
            for s in range(SPECIES):
                patch_send(d, s).wait_send()
                patch_wait(d, s).wait_recv()
            ghost_wait(d).wait_recv()


def smooth_kernel(
    nx, ny,
    src_s, mobility, fermi_gain, rates, conc, landp, landg, ghost_own,
    out,
    cur, ghost, coef, base, ping, pong, blank, cur_sem, ghost_sem, out_sem, zero_sem,
):
    gx, gy = lax.axis_index("gx"), lax.axis_index("gy")
    me = gx * ny + gy
    whence = []
    for t in range(KEEP):
        source = src_s[0, t]
        rel = source - me * CAP
        own = (rel >= 0) & (rel < CAP)
        came = jnp.int32(0)
        for d, step in enumerate(NEAR):
            away = source - (me + step[0] * ny + step[1]) * CAP
            came = jnp.where((away >= 0) & (away < CAP), d, came)
        whence.append((source, own, jnp.where(own, rel, 0), came))

    def fetch_own(t):
        return (
            pltpu.make_async_copy(
                conc.at[:, pl.ds(whence[t][2], 1), :], cur.at[t].reshape(SPECIES, 1, B**3), cur_sem.at[t]),
            pltpu.make_async_copy(ghost_own.at[t], ghost.at[t], ghost_sem.at[t]),
        )

    def fetch_moved(t):
        return (
            pltpu.make_async_copy(landp.at[whence[t][3]], cur.at[t], cur_sem.at[t]),
            pltpu.make_async_copy(landg.at[whence[t][3]], ghost.at[t], ghost_sem.at[t]),
        )

    for t in range(KEEP):
        source, own, slot, came = whence[t]

        @pl.when((source >= 0) & own)
        def _():
            for copy in fetch_own(t):
                copy.start()

        @pl.when((source >= 0) & jnp.logical_not(own))
        def _():
            for copy in fetch_moved(t):
                copy.start()

    blank[...] = jnp.zeros(blank.shape, jnp.float32)
    zeros = [
        pltpu.make_async_copy(blank, out.at[pl.ds(s, 1), pl.ds(KEEP, CAP - KEEP), :], zero_sem.at[s])
        for s in range(SPECIES)
    ]
    for copy in zeros:
        copy.start()
    lane = iota((8, 128), 1)
    sub = iota((8, 128), 0)
    z = lane % 32
    first_y = (sub == 0) & (lane < 32)
    last_y = (sub == 7) & (lane >= 96)

    def patch(t):
        for copy in fetch_moved(t):
            copy.wait()

        def prepare(xo, carry):
            for xi in range(8):
                x = xo * 8 + xi
                plane = pl.ds(pl.multiple_of(x * 8, 8), 8)
                a, i, v, p, q = [cur[t, s, plane, :] for s in range(SPECIES)]
                half = 0.5 * (a + p + q)
                electrons = half + jnp.sqrt(half * half + 1.0)
                ai = rates[0] * a * i - rates[1] * p
                av = rates[2] * a * v - rates[3] * q
                re = rates[4] * (i * v - 1.0)
                sources = (a - ai - av, i - ai - re, v - av - re, p + ai, q + av)
                for s in range(SPECIES):
                    gain = fermi_gain[s]
                    spread = mobility[s] * (1.0 + gain * electrons) / (1.0 + gain)
                    inverse = 1.0 / (1.0 + 6.0 * spread)
                    low = pltpu.roll(ghost[t, 4, s], (128 - x) % 128, 1)
                    high = pltpu.roll(ghost[t, 5, s], (31 - x + 128) % 128, 1)
                    extra = jnp.where(z == 0, low, 0.0) + jnp.where(z == 31, high, 0.0)
                    low = jnp.broadcast_to(ghost[t, 2, s, xi:xi + 1, :], (8, 128))
                    low = pltpu.roll(low, (128 - 32 * xo) % 128, 1)
                    high = jnp.broadcast_to(ghost[t, 3, s, xi:xi + 1, :], (8, 128))
                    high = pltpu.roll(high, (96 - 32 * xo) % 128, 1)
                    extra = extra + jnp.where(first_y, low, 0.0) + jnp.where(last_y, high, 0.0)
                    extra = extra + jnp.where(x == 0, ghost[t, 0, s], 0.0) + jnp.where(x == 31, ghost[t, 1, s], 0.0)
                    coef[s, plane, :] = spread * inverse
                    base[s, plane, :] = (sources[s] + spread * extra) * inverse
            return carry

        lax.fori_loop(0, 4, prepare, 0)

        def species(s, carry):
            def sweep(get, put):
                before = None
                here = get(0)
                for x in range(B):
                    after = get(x + 1) if x + 1 < B else None
                    total = jnp.where(z == 0, 0.0, pltpu.roll(here, 1, 1)) + jnp.where(z == 31, 0.0, pltpu.roll(here, 127, 1))
                    down = pltpu.roll(here, 32, 1)
                    down = jnp.where(lane >= 32, down, pltpu.roll(down, 1, 0))
                    up = pltpu.roll(here, 96, 1)
                    up = jnp.where(lane < 96, up, pltpu.roll(up, 7, 0))
                    total = total + jnp.where(first_y, 0.0, down) + jnp.where(last_y, 0.0, up)
                    if before is not None:
                        total = total + before
                    if after is not None:
                        total = total + after
                    put(x, base[s, 8 * x:8 * x + 8, :] + coef[s, 8 * x:8 * x + 8, :] * total)
                    before, here = here, after

            def put_ping(x, value):
                ping[8 * x:8 * x + 8, :] = value

            def put_last(x, value):
                pong[t, s, 8 * x:8 * x + 8, :] = value

            def put_pong(x, value):
                pong[t, s, 8 * x:8 * x + 8, :] = value

            sweep(lambda x: cur[t, s, 8 * x:8 * x + 8, :], put_pong)
            sweep(lambda x: pong[t, s, 8 * x:8 * x + 8, :], put_ping)
            sweep(lambda x: ping[8 * x:8 * x + 8, :], put_last)
            pltpu.make_async_copy(
                pong.at[t, pl.ds(s, 1)].reshape(1, 1, B**3), out.at[pl.ds(s, 1), pl.ds(t, 1), :], out_sem.at[t, s]
            ).start()
            return carry

        lax.fori_loop(0, SPECIES, species, 0)

    def put_out(t, s):
        return pltpu.make_async_copy(
            pong.at[t, pl.ds(s, 1)].reshape(1, 1, B**3), out.at[pl.ds(s, 1), pl.ds(t, 1), :], out_sem.at[t, s])

    for t in range(KEEP):
        @pl.when(src_s[0, t] >= 0)
        def _():
            patch(t)

        @pl.when(src_s[0, t] < 0)
        def _():
            pong[t] = jnp.zeros((SPECIES, ROWS, 128), jnp.float32)
            for s in range(SPECIES):
                put_out(t, s).start()
    for copy in zeros:
        copy.wait()
    for t in range(KEEP):
        for s in range(SPECIES):
            put_out(t, s).wait()


def in_vmem():
    return pl.BlockSpec(memory_space=pltpu.VMEM)


def in_smem():
    return pl.BlockSpec(memory_space=pltpu.SMEM)


def anywhere():
    return pl.BlockSpec(memory_space=pl.ANY)


def exchange(nx, ny, conc, neighbours, source):
    f32, i32 = jnp.float32, jnp.int32
    dma = pltpu.SemaphoreType.DMA
    n_flags = 3 + nx - 1 + 6
    return pl.pallas_call(
        functools.partial(exchange_kernel, nx, ny),
        out_shape=(
            jax.ShapeDtypeStruct((4, SPECIES, ROWS, 128), f32),
            jax.ShapeDtypeStruct((4, 6, SPECIES, 8, 128), f32),
            jax.ShapeDtypeStruct((KEEP, 6, SPECIES, 8, 128), f32),
            jax.ShapeDtypeStruct((8, 128), i32),
        ),
        in_specs=[anywhere(), in_smem(), in_smem(), in_vmem(), in_vmem()],
        out_specs=(anywhere(), anywhere(), in_vmem(), in_vmem()),
        scratch_shapes=[
            pltpu.VMEM((SPECIES, CAP, B**3), f32),
            pltpu.VMEM((CAP, SPECIES, ROWS, 128), f32),
            pltpu.VMEM((CAP * 6, SPECIES, 8, 128), f32),
            pltpu.VMEM((13, 8, 128), i32),
            pltpu.VMEM((5, 8, 128), i32),
            pltpu.SMEM((5, 8, 128), i32),
            pltpu.VMEM((4, SPECIES, ROWS, 128), f32),
            pltpu.VMEM((4, ROOM, SPECIES, 8, 128), f32),
            pltpu.VMEM((4, ROOM, SPECIES, 8, 128), f32),
            pltpu.VMEM((4, 6, SPECIES, 8, 128), f32),
            pltpu.VMEM((n_flags, 8, 128), i32),
            dma,
            dma((12,)), dma((12,)),
            dma,
            dma((4, SPECIES)), dma((4, SPECIES)), dma((4,)), dma((4,)), dma((4,)), dma((4,)),
            dma((n_flags,)), dma((n_flags,)),
        ],
        compiler_params=pltpu.CompilerParams(collective_id=0, has_side_effects=True, vmem_limit_bytes=40 * 2**20),
    )(conc, neighbours, source, neighbours, source)


def smooth(nx, ny, conc, landp, landg, ghost_own, source, mobility, fermi_gain, rates):
    f32 = jnp.float32
    dma = pltpu.SemaphoreType.DMA
    return pl.pallas_call(
        functools.partial(smooth_kernel, nx, ny),
        out_shape=jax.ShapeDtypeStruct((SPECIES, CAP, B**3), f32),
        in_specs=[in_smem()] * 4 + [anywhere()] * 4,
        out_specs=anywhere(),
        scratch_shapes=[
            pltpu.VMEM((KEEP, SPECIES, ROWS, 128), f32),
            pltpu.VMEM((KEEP, 6, SPECIES, 8, 128), f32),
            pltpu.VMEM((SPECIES, ROWS, 128), f32),
            pltpu.VMEM((SPECIES, ROWS, 128), f32),
            pltpu.VMEM((ROWS, 128), f32),
            pltpu.VMEM((KEEP, SPECIES, ROWS, 128), f32),
            pltpu.VMEM((1, CAP - KEEP, B**3), f32),
            dma((KEEP,)),
            dma((KEEP,)),
            dma((KEEP, SPECIES)),
            dma((SPECIES,)),
        ],
        compiler_params=pltpu.CompilerParams(vmem_limit_bytes=60 * 2**20),
    )(source, mobility, fermi_gain, rates, conc, landp, landg, ghost_own)


OPPOSITE = (1, 0, 3, 2, 5, 4)


def passed_along(x, axis, by):
    devices = lax.axis_size(axis)
    pairs = [(i, i + by) for i in range(devices) if 0 <= i + by < devices]
    return lax.ppermute(x, axis, pairs)


def with_halo(x, sides, width):
    edges = {}
    for axis, dim in sides:
        devices, length = (lax.axis_size(axis), x.shape[dim])
        up = [(i, (i + 1) % devices) for i in range(devices - 1)]
        last = lax.slice_in_dim(x, length - width, length, axis=dim)
        leading = lax.slice_in_dim(x, 0, width, axis=dim)
        edges[dim] = (
            lax.ppermute(last, axis, up),
            lax.ppermute(leading, axis, [(b, a) for a, b in up]),
        )
    done = []
    for _, dim in sides:
        low, high = edges[dim]
        around = [(width, width) if d in done else (0, 0) for d in range(x.ndim)]
        x = jnp.concatenate([jnp.pad(low, around), x, jnp.pad(high, around)], axis=dim)
        done.append(dim)
    return x


def faces_of(blocks):
    last = blocks.shape[-1] - 1
    return jnp.stack(
        [
            blocks[..., 0, :, :],
            blocks[..., last, :, :],
            blocks[..., :, 0, :],
            blocks[..., :, last, :],
            blocks[..., :, :, 0],
            blocks[..., :, :, last],
        ],
        axis=-4,
    )


def neighbour_sum(iterate, ghosts):
    lower_x = jnp.concatenate([ghosts[0][:, None], iterate[:, :-1]], axis=1)
    upper_x = jnp.concatenate([iterate[:, 1:], ghosts[1][:, None]], axis=1)
    lower_y = jnp.concatenate([ghosts[2][:, :, None], iterate[:, :, :-1]], axis=2)
    upper_y = jnp.concatenate([iterate[:, :, 1:], ghosts[3][:, :, None]], axis=2)
    lower_z = jnp.concatenate([ghosts[4][..., None], iterate[..., :-1]], axis=3)
    upper_z = jnp.concatenate([iterate[..., 1:], ghosts[5][..., None]], axis=3)
    return lower_x + upper_x + lower_y + upper_y + lower_z + upper_z


def smooth_plain(current, ghosts, mobility, fermi_gain, rates):
    dopant_sum = current[0] + current[3] + current[4]
    half_total = 0.5 * dopant_sum
    electrons = half_total + jnp.sqrt(half_total * half_total + 1.0)
    gain_column = fermi_gain[:, None, None, None]
    spread = (
        mobility[:, None, None, None] * (1.0 + gain_column * electrons[None]) / (1.0 + gain_column)
    )
    dopant, interstitial, vacancy, pair_inter, pair_vacancy = (
        current[0],
        current[1],
        current[2],
        current[3],
        current[4],
    )
    forming_ai = rates[0] * dopant * interstitial - rates[1] * pair_inter
    forming_av = rates[2] * dopant * vacancy - rates[3] * pair_vacancy
    recombine = rates[4] * (interstitial * vacancy - 1.0)
    source = jnp.stack(
        [
            dopant - forming_ai - forming_av,
            interstitial - forming_ai - recombine,
            vacancy - forming_av - recombine,
            pair_inter + forming_ai,
            pair_vacancy + forming_av,
        ],
        axis=0,
    )
    diagonal = 1.0 + 6.0 * spread
    iterate = current
    for repeat in range(SWEEPS):
        iterate = (source + spread * neighbour_sum(iterate, ghosts)) / diagonal
    return iterate


def smooth_all(current, ghosts, mobility, fermi_gain, rates):

    def per_patch(paired):
        return smooth_plain(paired[0], paired[1], mobility, fermi_gain, rates)

    return lax.map(per_patch, (current, ghosts))


def gather_ghosts(face_table, neighbours, column_index, row_index, rows_count, capacity):
    face_rows = face_table.reshape(9 * capacity * 6, SPECIES, B, B)
    safe_slot = jnp.maximum(neighbours, 0)
    source_device = safe_slot // capacity
    step_x = source_device // rows_count - column_index + 1
    step_y = source_device % rows_count - row_index + 1
    opposite = jnp.array(OPPOSITE, jnp.int32)
    face_ids = jnp.arange(6, dtype=jnp.int32)
    remote = ((step_x * 3 + step_y) * capacity + safe_slot % capacity) * 6 + opposite[None, :]
    local = (4 * capacity + jnp.arange(capacity, dtype=jnp.int32)[:, None]) * 6 + face_ids[None, :]
    picked = jnp.clip(jnp.where(neighbours >= 0, remote, local), 0, 9 * capacity * 6 - 1)
    one = functools.partial(lax.dynamic_index_in_dim, face_rows, axis=0, keepdims=False)
    ghosts = lax.map(one, picked.reshape(-1))
    return ghosts.reshape(picked.shape + face_rows.shape[1:])


def counted(hits):
    places = jnp.arange(hits.shape[0])
    before = places[None, :] <= places[:, None]
    return jnp.sum(jnp.where(before & hits[None, :], 1, 0), axis=1) - 1


def pick_rows(pulls, this_device, capacity, payload):
    wanted = (pulls >= 0) & (pulls // capacity == this_device)
    position = counted(wanted)
    chosen = wanted[None, :] & (position[None, :] == jnp.arange(MOVE, dtype=jnp.int32)[:, None])
    slot_list = jnp.sum(jnp.where(chosen, pulls % capacity, 0), axis=1)
    return payload[slot_list]


def place_rows(index, source_device, sender, start):
    from_sender = (source_device == sender) & (source_device >= 0)
    position = counted(from_sender)
    return jnp.where(from_sender, start + position, index)


def relocate(payload, source_slot, requests, this_device, rows_count, capacity):
    source_device = jnp.where(source_slot >= 0, source_slot // capacity, -1)
    index = jnp.where(
        (source_slot >= 0) & (source_device == this_device), source_slot % capacity, -1
    )
    pieces = [payload]
    start = capacity
    for offset in (1, -1):
        outgoing = pick_rows(requests[1 + offset, 1], this_device, capacity, payload)
        arrived = passed_along(outgoing, "gx", offset)
        index = place_rows(index, source_device, this_device - offset * rows_count, start)
        pieces.append(arrived)
        start = start + MOVE
    for offset in (1, -1):
        outgoing = pick_rows(requests[1, 1 + offset], this_device, capacity, payload)
        arrived = passed_along(outgoing, "gy", offset)
        index = place_rows(index, source_device, this_device - offset, start)
        pieces.append(arrived)
        start = start + MOVE
    candidates = jnp.concatenate(pieces, axis=0)
    gathered = candidates[jnp.maximum(index, 0)]
    return jnp.where((index >= 0)[:, None], gathered, jnp.zeros_like(gathered))


def general(concentration, neighbours, source_slot, mobility, fermi_gain, rates):
    capacity = concentration.shape[0]
    cells = concentration.shape[2]
    column_index = lax.axis_index("gx")
    row_index = lax.axis_index("gy")
    rows_count = lax.axis_size("gy")
    this_device = column_index * rows_count + row_index
    blocks = concentration.reshape(capacity, SPECIES, B, B, B)
    own_faces = faces_of(blocks).reshape(1, 1, capacity, 6, SPECIES, B * B)
    face_table = with_halo(own_faces, (("gx", 0), ("gy", 1)), 1)
    requests = with_halo(source_slot.reshape(1, 1, capacity), (("gx", 0), ("gy", 1)), 1)
    ghosts = gather_ghosts(face_table, neighbours, column_index, row_index, rows_count, capacity)
    working = KEEP - 1 + MOVE
    payload = jnp.concatenate(
        [
            concentration.reshape(capacity, SPECIES * cells),
            ghosts.reshape(capacity, 6 * SPECIES * B * B),
        ],
        axis=1,
    )
    arrived = relocate(payload, source_slot, requests, this_device, rows_count, capacity)[:working]
    current = arrived[:, : SPECIES * cells].reshape(working, SPECIES, B, B, B)
    layers = arrived[:, SPECIES * cells :].reshape(working, 6, SPECIES, B, B)
    swept = smooth_all(current, layers, mobility, fermi_gain, rates).reshape(
        working, SPECIES, cells
    )
    live_rows = (source_slot[:working] >= 0)[:, None, None]
    swept = jnp.where(live_rows, swept, jnp.zeros_like(swept))
    return jnp.concatenate(
        [swept, jnp.zeros((capacity - working, SPECIES, cells), jnp.float32)], axis=0
    )


def body(nx, ny, concentration, neighbours, source_slot, mobility, fermi_gain, rates):
    source = source_slot.reshape(1, CAP)
    conc = concentration.transpose(1, 0, 2)
    landp, landg, ghost, flag = exchange(nx, ny, conc, neighbours, source)

    def common():
        return smooth(nx, ny, conc, landp, landg, ghost, source, mobility, fermi_gain, rates).transpose(1, 0, 2)

    def crowded():
        return general(concentration, neighbours, source_slot, mobility, fermi_gain, rates)

    return lax.cond(flag[0, 0] == 0, common, crowded)


def solution(mesh):
    placed = (P(("gx", "gy"), None, None), P(("gx", "gy"), None), P(("gx", "gy")), P(), P(), P())
    return jax.shard_map(
        functools.partial(body, mesh.shape["gx"], mesh.shape["gy"]),
        mesh=mesh, in_specs=placed, out_specs=P(("gx", "gy"), None, None), check_vma=False,
    )
```

profile of v0, /device:TPU:0, one launch (start us, length us, event | category | flops | bytes accessed | tf_op | source)
XLA Modules:
  0.0 54.0 jit_solution(1659560556598010353)
XLA Ops:
  0.0 0.0 copy-start.12
  0.0 0.0 copy-start.13
  0.0 42.3 %shard_map.76 = (f32[4,5,256,128]{3,2,1,0:T(8,128)}, f32[4,6,5,8,128]{4,3,2,1,0:T(8,128)}, f32[2,6,5,8,128]{4,3,2,1,0:T(8,128)}, s32[8,128]{1,0:T(8,128)S(1)}) custom-call(f32[5,6,32768]{2,1,0:T(8,128)} %bitcast.373, s32[6,6]{1,0:T(8,128)} %nbr_v.1, s32[1,6]{1,0:T(1,128)} %bitcast.383, s32[6,6]{1,0:T(8,128)} %nbr_v.1, s32[1,6]{1,0:T(1,128)} %bitcast.384), custom_call_target="tpu_custom_call" | custom-call | tf_op jit(solution)/shard_map/pallas_call | solution.py:493
  42.3 0.5 slice.265
  43.5 0.0 copy-done.12
  43.5 0.0 copy-done.13
  43.5 10.3 %conditional.1 = (f32[6,5,32768]{2,0,1:T(8,128)}) conditional(s32[]{:T(128)} %bitcast.92, (s32[6]{0:T(128)S(1)}, f32[6,5,32768]{2,0,1:T(8,128)}, s32[6,6]{1,0:T(8,128)S(1)}, (), f32[5]{0:T(128)}, /*index=5*/f32[5]{0:T(128)}, f32[5]{0:T(128)}) %tuple.146, (s32[1,6]{1,0:T(1,128)S(1)}, f32[5]{0:T(128)}, f32[5]{0:T(128)}, f32[5]{0:T(128)}, ...), branch_computations={%region_0.17_spmd, %region_17.18_spmd} | conditional | flops 29352638 | bytes 266848192 | solution.py:751
  43.7 10.1 %branch_1_fun.1 = f32[5,6,32768]{2,1,0:T(8,128)} custom-call(s32[1,6]{1,0:T(1,128)S(1)} %get-tuple-element.156.src_s, f32[5]{0:T(128)} %get-tuple-element.157.mobility, f32[5]{0:T(128)} %get-tuple-element.158.fermi_gain, f32[5]{0:T(128)} %get-tuple-element.159.rates, f32[5,6,32768]{2,1,0:T(8,128)} %get-tuple-element.160.conc, ...), custom_call_target="tpu_custom_call" | custom-call | tf_op jit(solution)/shard_map/cond/branch_1_fun/pallas_call | solution.py:528
Async XLA Ops:
  0.0 43.5 %copy-start.12 = (s32[6,6]{1,0:T(8,128)S(1)}, s32[6,6]{1,0:T(8,128)}, u32[]{:S(2)}) copy-start(s32[6,6]{1,0:T(8,128)} %nbr_v.1) | copy-start | bytes 436
  0.0 43.5 %copy-start.13 = (s32[6]{0:T(128)S(1)}, s32[6]{0:T(128)}, u32[]{:S(2)}) copy-start(s32[6]{0:T(128)} %param.15) | copy-start | bytes 76
where the time goes:
time: 54.2 us; the launch traced here: 54 us
  Pallas kernels  52.3 us (96%)
  between operations  0.86 us (2%)
    pallas_call x1, Pallas kernels, exchange(): pl.pallas_call(functools.partial(exchange_kernel, nx, ny), out_shape=(jax...  42.3 us
    pallas_call x1, Pallas kernels, smooth(): pl.pallas_call(functools.partial(smooth_kernel, nx, ny), out_shape=jax.Sh...  10.1 us

commit v1 on v0

--- a/solution.py
+++ b/solution.py
@@ -14,6 +14,7 @@
 MOVE = 1
 CAP = 6
 ROWS = 256
+EARLY = 12
 ROOM = 6
 MESH = pl.DeviceIdType.MESH
 
@@ -28,12 +29,88 @@
     return lax.broadcasted_iota(jnp.int32, shape, dim)
 
 
+def step_patch(mobility, fermi_gain, rates, cell, layer, coef, base, ping, result, finish):
+    lane = iota((8, 128), 1)
+    sub = iota((8, 128), 0)
+    z = lane % 32
+    first_y = (sub == 0) & (lane < 32)
+    last_y = (sub == 7) & (lane >= 96)
+    whole = pl.ds(0, 8)
+    scale = [mobility[s] / jnp.full((8, 128), 1.0 + fermi_gain[s]) for s in range(SPECIES)]
+
+    def prepare(xo, carry):
+        for xi in range(8):
+            x = xo * 8 + xi
+            plane = pl.ds(pl.multiple_of(x * 8, 8), 8)
+            a, i, v, p, q = [cell(s, plane) for s in range(SPECIES)]
+            half = 0.5 * (a + p + q)
+            electrons = half + jnp.sqrt(half * half + 1.0)
+            ai = rates[0] * a * i - rates[1] * p
+            av = rates[2] * a * v - rates[3] * q
+            re = rates[4] * (i * v - 1.0)
+            sources = (a - ai - av, i - ai - re, v - av - re, p + ai, q + av)
+            for s in range(SPECIES):
+                spread = scale[s] * (1.0 + fermi_gain[s] * electrons)
+                inverse = 1.0 / (1.0 + 6.0 * spread)
+                low = pltpu.roll(layer(4, s, whole), (128 - x) % 128, 1)
+                high = pltpu.roll(layer(5, s, whole), (31 - x + 128) % 128, 1)
+                extra = jnp.where(z == 0, low, jnp.where(z == 31, high, 0.0))
+                low = jnp.broadcast_to(layer(2, s, pl.ds(xi, 1)), (8, 128))
+                high = jnp.broadcast_to(layer(3, s, pl.ds(xi, 1)), (8, 128))
+                low = pltpu.roll(low, (128 - 32 * xo) % 128, 1)
+                high = pltpu.roll(high, (96 - 32 * xo) % 128, 1)
+                extra = extra + jnp.where(first_y, low, jnp.where(last_y, high, 0.0))
+                if xi == 0:
+                    extra = extra + jnp.where(x == 0, layer(0, s, whole), 0.0)
+                if xi == 7:
+                    extra = extra + jnp.where(x == B - 1, layer(1, s, whole), 0.0)
+                weight = spread * inverse
+                coef[s, plane, :] = weight
+                base[s, plane, :] = sources[s] * inverse + weight * extra
+        return carry
+
+    lax.fori_loop(0, 4, prepare, 0)
+
+    def species(s, carry):
+        def sweep(get, put):
+            before = None
+            here = get(0)
+            for x in range(B):
+                after = get(x + 1) if x + 1 < B else None
+                total = jnp.where(z == 0, 0.0, pltpu.roll(here, 1, 1)) + jnp.where(z == 31, 0.0, pltpu.roll(here, 127, 1))
+                down = pltpu.roll(here, 32, 1)
+                down = jnp.where(lane >= 32, down, pltpu.roll(down, 1, 0))
+                up = pltpu.roll(here, 96, 1)
+                up = jnp.where(lane < 96, up, pltpu.roll(up, 7, 0))
+                total = total + jnp.where(first_y, 0.0, down) + jnp.where(last_y, 0.0, up)
+                if before is not None:
+                    total = total + before
+                if after is not None:
+                    total = total + after
+                put(x, base[s, 8 * x:8 * x + 8, :] + coef[s, 8 * x:8 * x + 8, :] * total)
+                before, here = here, after
+
+        def put_ping(x, value):
+            ping[8 * x:8 * x + 8, :] = value
+
+        def put_result(x, value):
+            result[s, 8 * x:8 * x + 8, :] = value
+
+        sweep(lambda x: cell(s, pl.ds(8 * x, 8)), put_result)
+        sweep(lambda x: result[s, 8 * x:8 * x + 8, :], put_ping)
+        sweep(lambda x: ping[8 * x:8 * x + 8, :], put_result)
+        finish(s)
+        return carry
+
+    lax.fori_loop(0, SPECIES, species, 0)
+
+
 def exchange_kernel(
     nx, ny,
-    conc, nbr_s, src_s, nbr_v, src_v,
-    landp, landg, ghost_out, flag_out,
-    raw, dense, own_faces, meta, table, table_s, sendp, sendf, landf, sendg, flags,
-    in_sem, meta_ss, meta_rs, tab_sem, p_ss, p_rs, f_ss, f_rs, g_ss, g_rs, fl_ss, fl_rs,
+    conc, nbr_s, src_s, mobility, fermi_gain, rates, nbr_v, src_v,
+    landp, landg, swept, flag_out,
+    raw, dense, own_faces, meta, table, table_s, sendp, sendf, landf, sendg, flags, ghost, coef, base, ping, result,
+    in_sem, meta_ss, meta_rs, tab_sem, p_ss, p_rs, f_ss, f_rs, g_ss, g_rs, fl_ss, fl_rs, out_sem,
 ):
     gx, gy = lax.axis_index("gx"), lax.axis_index("gy")
     me = gx * ny + gy
@@ -50,9 +127,9 @@
 
     row, col = gy // 4, gy % 4
     ring = (
+        [(gx, row * 4 + (col + k) % 4) for k in range(1, 4)],
         [((gx + k) % nx, gy) for k in range(1, nx)],
         [(gx, ((row + k) % 4) * 4 + col) for k in range(1, 4)],
-        [(gx, row * 4 + (col + k) % 4) for k in range(1, 4)],
     )
 
     meta[...] = jnp.full(meta.shape, -1, jnp.int32)
@@ -81,21 +158,6 @@
         return carry
 
     lax.fori_loop(0, SPECIES * B, spread_out, 0)
-
-    pl.semaphore_wait(barrier, expected)
-
-    def opposite(i):
-        return AROUND.index((-AROUND[i][0], -AROUND[i][1]))
-
-    def meta_send(i):
-        return pltpu.make_async_remote_copy(
-            src_ref=meta.at[0], dst_ref=meta.at[1 + opposite(i)],
-            send_sem=meta_ss.at[i], recv_sem=meta_rs.at[opposite(i)], device_id=at(AROUND[i]), device_id_type=MESH)
-
-    for i, step in enumerate(AROUND):
-        @pl.when(inside(step))
-        def _():
-            meta_send(i).start()
 
     lane8 = iota((8, 128), 1)
 
@@ -123,7 +185,23 @@
         own_faces[q * 6 + 5, s] = pltpu.roll(high, 96, 1)
         return carry
 
-    lax.fori_loop(0, CAP * SPECIES, faces, 0)
+    lax.fori_loop(0, EARLY, faces, 0)
+    pl.semaphore_wait(barrier, expected)
+
+    def opposite(i):
+        return AROUND.index((-AROUND[i][0], -AROUND[i][1]))
+
+    def meta_send(i):
+        return pltpu.make_async_remote_copy(
+            src_ref=meta.at[0], dst_ref=meta.at[1 + opposite(i)],
+            send_sem=meta_ss.at[i], recv_sem=meta_rs.at[opposite(i)], device_id=at(AROUND[i]), device_id_type=MESH)
+
+    for i, step in enumerate(AROUND):
+        @pl.when(inside(step))
+        def _():
+            meta_send(i).start()
+
+    lax.fori_loop(EARLY, CAP * SPECIES, faces, 0)
 
     for i, step in enumerate(AROUND):
         @pl.when(inside(step))
@@ -230,6 +308,16 @@
     to_scalars = pltpu.make_async_copy(table, table_s, tab_sem)
     to_scalars.start()
 
+    def flag_copy(base, k, target, held):
+        return pltpu.make_async_remote_copy(
+            src_ref=flags.at[held], dst_ref=flags.at[base + k], send_sem=fl_ss.at[base + k],
+            recv_sem=fl_rs.at[base + k], device_id=target, device_id_type=MESH)
+
+    bases = (3, 6, 6 + nx - 1)
+
+    for k, target in enumerate(ring[0]):
+        flag_copy(bases[0], k, target, 0).start()
+
     to_scalars.wait()
     for d in ORDER:
         @pl.when(inside(NEAR[d]))
@@ -240,15 +328,23 @@
             lax.fori_loop(0, ROOM, stage, 0)
             face_send(d).start()
 
-    def flag_copy(base, k, target, held):
-        return pltpu.make_async_remote_copy(
-            src_ref=flags.at[held], dst_ref=flags.at[base + k], send_sem=fl_ss.at[base + k],
-            recv_sem=fl_rs.at[base + k], device_id=target, device_id_type=MESH)
-
-    bases = (3, 3 + nx - 1, 3 + nx - 1 + 3)
-    for k, target in enumerate(ring[0]):
-        flag_copy(bases[0], k, target, 0).start()
     patches((1, 2, 3, 4))
+
+    def flag_round(n, held, following):
+        for k, target in enumerate(ring[n]):
+            copy = flag_copy(bases[n], k, target, held)
+            copy.wait()
+        total = flags[held]
+        for k in range(len(ring[n])):
+            total = jnp.maximum(total, flags[bases[n] + k])
+        if following is None:
+            flag_out[...] = total
+        else:
+            flags[following] = total
+            for k, target in enumerate(ring[n + 1]):
+                flag_copy(bases[n + 1], k, target, following).start()
+
+    flag_round(0, 0, 1)
 
     for d, step in enumerate(NEAR):
         @pl.when(inside(step))
@@ -284,32 +380,25 @@
             lax.fori_loop(0, 6, stage, 0)
             ghost_send(d).start()
 
-    def flag_round(n, held, following):
-        for k, target in enumerate(ring[n]):
-            copy = flag_copy(bases[n], k, target, held)
-            copy.wait()
-        total = flags[held]
-        for k in range(len(ring[n])):
-            total = jnp.maximum(total, flags[bases[n] + k])
-        if following is None:
-            flag_out[...] = total
-        else:
-            flags[following] = total
-            for k, target in enumerate(ring[n + 1]):
-                flag_copy(bases[n + 1], k, target, following).start()
-
-    flag_round(0, 0, 1)
-
-    for t in range(KEEP):
+    flag_round(1, 1, 2)
+
+    def stay(t, carry):
         rel = src_s[0, t] - me * CAP
         slot = jnp.where((rel >= 0) & (rel < CAP), rel, 0)
 
         def layer(f, carry):
-            ghost_out[t, f] = ghost_value(slot, f)
+            ghost[f] = ghost_value(slot, f)
             return carry
         lax.fori_loop(0, 6, layer, 0)
-
-    flag_round(1, 1, 2)
+        step_patch(
+            mobility, fermi_gain, rates,
+            lambda s, rows: dense[slot, s, rows, :], lambda f, s, rows: ghost[f, s, rows, :],
+            coef, base, ping, result.at[t], lambda s: None)
+        pltpu.make_async_copy(result.at[t], swept.at[t], out_sem.at[t]).start()
+        return carry
+
+    lax.fori_loop(0, KEEP, stay, 0)
+
     flag_round(2, 2, None)
 
     for d, step in enumerate(NEAR):
@@ -321,11 +410,13 @@
                 patch_send(d, s).wait_send()
                 patch_wait(d, s).wait_recv()
             ghost_wait(d).wait_recv()
+    for t in range(KEEP):
+        pltpu.make_async_copy(result.at[t], swept.at[t], out_sem.at[t]).wait()
 
 
 def smooth_kernel(
     nx, ny,
-    src_s, mobility, fermi_gain, rates, conc, landp, landg, ghost_own,
+    src_s, mobility, fermi_gain, rates, landp, landg, swept,
     out,
     cur, ghost, coef, base, ping, pong, blank, cur_sem, ghost_sem, out_sem, zero_sem,
 ):
@@ -343,11 +434,7 @@
         whence.append((source, own, jnp.where(own, rel, 0), came))
 
     def fetch_own(t):
-        return (
-            pltpu.make_async_copy(
-                conc.at[:, pl.ds(whence[t][2], 1), :], cur.at[t].reshape(SPECIES, 1, B**3), cur_sem.at[t]),
-            pltpu.make_async_copy(ghost_own.at[t], ghost.at[t], ghost_sem.at[t]),
-        )
+        return (pltpu.make_async_copy(swept.at[t], pong.at[t], cur_sem.at[t]),)
 
     def fetch_moved(t):
         return (
@@ -375,98 +462,38 @@
     ]
     for copy in zeros:
         copy.start()
-    lane = iota((8, 128), 1)
-    sub = iota((8, 128), 0)
-    z = lane % 32
-    first_y = (sub == 0) & (lane < 32)
-    last_y = (sub == 7) & (lane >= 96)
-
-    def patch(t):
-        for copy in fetch_moved(t):
-            copy.wait()
-
-        def prepare(xo, carry):
-            for xi in range(8):
-                x = xo * 8 + xi
-                plane = pl.ds(pl.multiple_of(x * 8, 8), 8)
-                a, i, v, p, q = [cur[t, s, plane, :] for s in range(SPECIES)]
-                half = 0.5 * (a + p + q)
-                electrons = half + jnp.sqrt(half * half + 1.0)
-                ai = rates[0] * a * i - rates[1] * p
-                av = rates[2] * a * v - rates[3] * q
-                re = rates[4] * (i * v - 1.0)
-                sources = (a - ai - av, i - ai - re, v - av - re, p + ai, q + av)
-                for s in range(SPECIES):
-                    gain = fermi_gain[s]
-                    spread = mobility[s] * (1.0 + gain * electrons) / (1.0 + gain)
-                    inverse = 1.0 / (1.0 + 6.0 * spread)
-                    low = pltpu.roll(ghost[t, 4, s], (128 - x) % 128, 1)
-                    high = pltpu.roll(ghost[t, 5, s], (31 - x + 128) % 128, 1)
-                    extra = jnp.where(z == 0, low, 0.0) + jnp.where(z == 31, high, 0.0)
-                    low = jnp.broadcast_to(ghost[t, 2, s, xi:xi + 1, :], (8, 128))
-                    low = pltpu.roll(low, (128 - 32 * xo) % 128, 1)
-                    high = jnp.broadcast_to(ghost[t, 3, s, xi:xi + 1, :], (8, 128))
-                    high = pltpu.roll(high, (96 - 32 * xo) % 128, 1)
-                    extra = extra + jnp.where(first_y, low, 0.0) + jnp.where(last_y, high, 0.0)
-                    extra = extra + jnp.where(x == 0, ghost[t, 0, s], 0.0) + jnp.where(x == 31, ghost[t, 1, s], 0.0)
-                    coef[s, plane, :] = spread * inverse
-                    base[s, plane, :] = (sources[s] + spread * extra) * inverse
-            return carry
-
-        lax.fori_loop(0, 4, prepare, 0)
-
-        def species(s, carry):
-            def sweep(get, put):
-                before = None
-                here = get(0)
-                for x in range(B):
-                    after = get(x + 1) if x + 1 < B else None
-                    total = jnp.where(z == 0, 0.0, pltpu.roll(here, 1, 1)) + jnp.where(z == 31, 0.0, pltpu.roll(here, 127, 1))
-                    down = pltpu.roll(here, 32, 1)
-                    down = jnp.where(lane >= 32, down, pltpu.roll(down, 1, 0))
-                    up = pltpu.roll(here, 96, 1)
-                    up = jnp.where(lane < 96, up, pltpu.roll(up, 7, 0))
-                    total = total + jnp.where(first_y, 0.0, down) + jnp.where(last_y, 0.0, up)
-                    if before is not None:
-                        total = total + before
-                    if after is not None:
-                        total = total + after
-                    put(x, base[s, 8 * x:8 * x + 8, :] + coef[s, 8 * x:8 * x + 8, :] * total)
-                    before, here = here, after
-
-            def put_ping(x, value):
-                ping[8 * x:8 * x + 8, :] = value
-
-            def put_last(x, value):
-                pong[t, s, 8 * x:8 * x + 8, :] = value
-
-            def put_pong(x, value):
-                pong[t, s, 8 * x:8 * x + 8, :] = value
-
-            sweep(lambda x: cur[t, s, 8 * x:8 * x + 8, :], put_pong)
-            sweep(lambda x: pong[t, s, 8 * x:8 * x + 8, :], put_ping)
-            sweep(lambda x: ping[8 * x:8 * x + 8, :], put_last)
-            pltpu.make_async_copy(
-                pong.at[t, pl.ds(s, 1)].reshape(1, 1, B**3), out.at[pl.ds(s, 1), pl.ds(t, 1), :], out_sem.at[t, s]
-            ).start()
-            return carry
-
-        lax.fori_loop(0, SPECIES, species, 0)
-
     def put_out(t, s):
         return pltpu.make_async_copy(
             pong.at[t, pl.ds(s, 1)].reshape(1, 1, B**3), out.at[pl.ds(s, 1), pl.ds(t, 1), :], out_sem.at[t, s])
 
     for t in range(KEEP):
-        @pl.when(src_s[0, t] >= 0)
-        def _():
-            patch(t)
-
-        @pl.when(src_s[0, t] < 0)
+        source, own, slot, came = whence[t]
+
+        @pl.when(source < 0)
         def _():
             pong[t] = jnp.zeros((SPECIES, ROWS, 128), jnp.float32)
             for s in range(SPECIES):
                 put_out(t, s).start()
+
+        @pl.when((source >= 0) & own)
+        def _():
+            for copy in fetch_own(t):
+                copy.wait()
+            for s in range(SPECIES):
+                put_out(t, s).start()
+
+    for t in range(KEEP):
+        source, own, slot, came = whence[t]
+
+        @pl.when((source >= 0) & jnp.logical_not(own))
+        def _():
+            for copy in fetch_moved(t):
+                copy.wait()
+            step_patch(
+                mobility, fermi_gain, rates,
+                lambda s, rows: cur[t, s, rows, :], lambda f, s, rows: ghost[t, f, s, rows, :],
+                coef, base, ping, pong.at[t], lambda s: put_out(t, s).start())
+
     for copy in zeros:
         copy.wait()
     for t in range(KEEP):
@@ -486,7 +513,7 @@
     return pl.BlockSpec(memory_space=pl.ANY)
 
 
-def exchange(nx, ny, conc, neighbours, source):
+def exchange(nx, ny, conc, neighbours, source, mobility, fermi_gain, rates):
     f32, i32 = jnp.float32, jnp.int32
     dma = pltpu.SemaphoreType.DMA
     n_flags = 3 + nx - 1 + 6
@@ -495,11 +522,11 @@
         out_shape=(
             jax.ShapeDtypeStruct((4, SPECIES, ROWS, 128), f32),
             jax.ShapeDtypeStruct((4, 6, SPECIES, 8, 128), f32),
-            jax.ShapeDtypeStruct((KEEP, 6, SPECIES, 8, 128), f32),
+            jax.ShapeDtypeStruct((KEEP, SPECIES, ROWS, 128), f32),
             jax.ShapeDtypeStruct((8, 128), i32),
         ),
-        in_specs=[anywhere(), in_smem(), in_smem(), in_vmem(), in_vmem()],
-        out_specs=(anywhere(), anywhere(), in_vmem(), in_vmem()),
+        in_specs=[anywhere()] + [in_smem()] * 5 + [in_vmem()] * 2,
+        out_specs=(anywhere(), anywhere(), anywhere(), in_vmem()),
         scratch_shapes=[
             pltpu.VMEM((SPECIES, CAP, B**3), f32),
             pltpu.VMEM((CAP, SPECIES, ROWS, 128), f32),
@@ -512,23 +539,29 @@
             pltpu.VMEM((4, ROOM, SPECIES, 8, 128), f32),
             pltpu.VMEM((4, 6, SPECIES, 8, 128), f32),
             pltpu.VMEM((n_flags, 8, 128), i32),
+            pltpu.VMEM((6, SPECIES, 8, 128), f32),
+            pltpu.VMEM((SPECIES, ROWS, 128), f32),
+            pltpu.VMEM((SPECIES, ROWS, 128), f32),
+            pltpu.VMEM((ROWS, 128), f32),
+            pltpu.VMEM((KEEP, SPECIES, ROWS, 128), f32),
             dma,
             dma((12,)), dma((12,)),
             dma,
             dma((4, SPECIES)), dma((4, SPECIES)), dma((4,)), dma((4,)), dma((4,)), dma((4,)),
             dma((n_flags,)), dma((n_flags,)),
+            dma((KEEP,)),
         ],
         compiler_params=pltpu.CompilerParams(collective_id=0, has_side_effects=True, vmem_limit_bytes=40 * 2**20),
-    )(conc, neighbours, source, neighbours, source)
-
-
-def smooth(nx, ny, conc, landp, landg, ghost_own, source, mobility, fermi_gain, rates):
+    )(conc, neighbours, source, mobility, fermi_gain, rates, neighbours, source)
+
+
+def smooth(nx, ny, landp, landg, swept, source, mobility, fermi_gain, rates):
     f32 = jnp.float32
     dma = pltpu.SemaphoreType.DMA
     return pl.pallas_call(
         functools.partial(smooth_kernel, nx, ny),
         out_shape=jax.ShapeDtypeStruct((SPECIES, CAP, B**3), f32),
-        in_specs=[in_smem()] * 4 + [anywhere()] * 4,
+        in_specs=[in_smem()] * 4 + [anywhere()] * 3,
         out_specs=anywhere(),
         scratch_shapes=[
             pltpu.VMEM((KEEP, SPECIES, ROWS, 128), f32),
@@ -544,7 +577,7 @@
             dma((SPECIES,)),
         ],
         compiler_params=pltpu.CompilerParams(vmem_limit_bytes=60 * 2**20),
-    )(source, mobility, fermi_gain, rates, conc, landp, landg, ghost_own)
+    )(source, mobility, fermi_gain, rates, landp, landg, swept)
 
 
 OPPOSITE = (1, 0, 3, 2, 5, 4)
@@ -740,10 +773,10 @@
 def body(nx, ny, concentration, neighbours, source_slot, mobility, fermi_gain, rates):
     source = source_slot.reshape(1, CAP)
     conc = concentration.transpose(1, 0, 2)
-    landp, landg, ghost, flag = exchange(nx, ny, conc, neighbours, source)
+    landp, landg, swept, flag = exchange(nx, ny, conc, neighbours, source, mobility, fermi_gain, rates)
 
     def common():
-        return smooth(nx, ny, conc, landp, landg, ghost, source, mobility, fermi_gain, rates).transpose(1, 0, 2)
+        return smooth(nx, ny, landp, landg, swept, source, mobility, fermi_gain, rates).transpose(1, 0, 2)
 
     def crowded():
         return general(concentration, neighbours, source_slot, mobility, fermi_gain, rates)

time: 54.2 us -> 47.7 us (0.88)
  the two profiles are of different devices: /device:TPU:0 before, /device:TPU:11 now
where the time goes in v1:
time: 47.7 us; the launch traced here: 47.5 us
  Pallas kernels  45.8 us (96%)
  between operations  0.86 us (2%)
  local copies, waits for them, and re-layouts  0.52 us (1%)
    pallas_call x1, Pallas kernels, exchange(): pl.pallas_call(functools.partial(exchange_kernel, nx, ny), out_shape=(jax...  38.6 us
    pallas_call x1, Pallas kernels, smooth(): pl.pallas_call(functools.partial(smooth_kernel, nx, ny), out_shape=jax.Sh...  7.2 us

profile of v1, /device:TPU:11, one launch (start us, length us, event | category | flops | bytes accessed | tf_op | source)
XLA Modules:
  0.0 47.5 jit_solution(582137797455520658)
XLA Ops:
  0.0 0.0 copy-start.12
  0.0 0.0 copy-start.13
  0.0 38.6 %shard_map.76 = (f32[4,5,256,128]{3,2,1,0:T(8,128)}, f32[4,6,5,8,128]{4,3,2,1,0:T(8,128)}, f32[2,5,256,128]{3,2,1,0:T(8,128)}, s32[8,128]{1,0:T(8,128)S(1)}) custom-call(f32[5,6,32768]{2,1,0:T(8,128)} %bitcast.373, s32[6,6]{1,0:T(8,128)} %nbr_v.1, s32[1,6]{1,0:T(1,128)} %bitcast.382, f32[5]{0:T(128)} %mobility.1, f32[5]{0:T(128)} %fermi_gain.1, f32[5]{0:T(128)} %rates.1, ...), custom_call_target="tpu_custom_call" | custom-call | tf_op jit(solution)/shard_map/pallas_call | solution.py:520
  38.6 0.5 %slice.265 = s32[1,1]{1,0:T(1,128)} slice(s32[8,128]{1,0:T(8,128)S(1)} %get-tuple-element.165), slice={[0:1], [0:1]} | slice | bytes 8 | tf_op jit(solution)/shard_map/slice | solution.py:784
  39.8 0.0 copy-done.12
  39.8 0.0 copy-done.13
  39.8 7.4 %conditional.1 = (f32[6,5,32768]{2,0,1:T(8,128)}) conditional(s32[]{:T(128)} %bitcast.92, (s32[6]{0:T(128)S(1)}, f32[6,5,32768]{2,0,1:T(8,128)}, s32[6,6]{1,0:T(8,128)S(1)}, (), f32[5]{0:T(128)}, /*index=5*/f32[5]{0:T(128)}, f32[5]{0:T(128)}) %tuple.145, (s32[1,6]{1,0:T(1,128)S(1)}, f32[5]{0:T(128)}, f32[5]{0:T(128)}, f32[5]{0:T(128)}, ...), branch_computations={%region_0.17_spmd, %region_17.18_spmd} | conditional | flops 29352638 | bytes 266848192 | solution.py:784
  40.1 7.2 %branch_1_fun.1 = f32[5,6,32768]{2,1,0:T(8,128)} custom-call(s32[1,6]{1,0:T(1,128)S(1)} %get-tuple-element.154.src_s, f32[5]{0:T(128)} %get-tuple-element.155.mobility, f32[5]{0:T(128)} %get-tuple-element.156.fermi_gain, f32[5]{0:T(128)} %get-tuple-element.157.rates, f32[4,5,256,128]{3,2,1,0:T(8,128)} %get-tuple-element.158.landp, ...), custom_call_target="tpu_custom_call" | custom-call | tf_op jit(solution)/shard_map/cond/branch_1_fun/pallas_call | solution.py:561
Async XLA Ops:
  0.0 39.8 %copy-start.12 = (s32[6,6]{1,0:T(8,128)S(1)}, s32[6,6]{1,0:T(8,128)}, u32[]{:S(2)}) copy-start(s32[6,6]{1,0:T(8,128)} %nbr_v.1) | copy-start | bytes 436
  0.0 39.8 %copy-start.13 = (s32[6]{0:T(128)S(1)}, s32[6]{0:T(128)}, u32[]{:S(2)}) copy-start(s32[6]{0:T(128)} %param.15) | copy-start | bytes 76

commit v2 on v1

--- a/solution.py
+++ b/solution.py
@@ -22,6 +22,7 @@
 FAR = ((-2, 0), (2, 0), (0, -2), (0, 2), (-1, -1), (-1, 1), (1, -1), (1, 1))
 AROUND = NEAR + FAR
 ORDER = (2, 3, 0, 1)
+HALF = ROWS // 2
 PLACE = {(0, 0): 0, **{step: i + 1 for i, step in enumerate(AROUND)}}
 
 
@@ -108,9 +109,9 @@
 def exchange_kernel(
     nx, ny,
     conc, nbr_s, src_s, mobility, fermi_gain, rates, nbr_v, src_v,
-    landp, landg, swept, flag_out,
-    raw, dense, own_faces, meta, table, table_s, sendp, sendf, landf, sendg, flags, ghost, coef, base, ping, result,
-    in_sem, meta_ss, meta_rs, tab_sem, p_ss, p_rs, f_ss, f_rs, g_ss, g_rs, fl_ss, fl_rs, out_sem,
+    landp, landz, landq, landg, swept, flag_out,
+    raw, dense, own_faces, meta, table, table_s, sendp, sendq, heldq, sendz, sendf, landf, sendg, flags, ghost, coef, base, ping, result,
+    in_sem, meta_ss, meta_rs, tab_sem, p_ss, p_rs, q_ss, q_rs, z_ss, z_rs, h_ss, h_rs, f_ss, f_rs, g_ss, g_rs, fl_ss, fl_rs, out_sem,
 ):
     gx, gy = lax.axis_index("gx"), lax.axis_index("gy")
     me = gx * ny + gy
@@ -223,6 +224,7 @@
         slot = jnp.max(jnp.where((rel >= 0) & (rel < CAP), rel, -1))
         taken.append(slot)
     safe = [jnp.maximum(slot, 0) for slot in taken]
+    asked = [slot >= 0 for slot in taken]
 
     def patch_send(d, s):
         return pltpu.make_async_remote_copy(
@@ -234,19 +236,47 @@
             src_ref=sendp.at[d, s], dst_ref=landp.at[d, s], send_sem=p_ss.at[d, s], recv_sem=p_rs.at[d, s],
             device_id=at(NEAR[d]), device_id_type=MESH)
 
-    def patches(some):
-        for d in ORDER:
+    def stage(to, slot, s, first, rows):
+        def part(r, carry):
+            to[pl.ds(pl.multiple_of(r * 64, 64), 64), :] = dense[slot, s, pl.ds(pl.multiple_of(first + r * 64, 64), 64), :]
+            return carry
+        lax.fori_loop(0, rows // 64, part, 0)
+
+    core = gx % 2
+    twin = (gx + 1 - 2 * core, gy)
+    mine_first, twin_first = core * HALF, (1 - core) * HALF
+
+    def copy_along(src, dst, ss, rs, target):
+        return pltpu.make_async_remote_copy(
+            src_ref=src, dst_ref=dst, send_sem=ss, recv_sem=rs, device_id=target, device_id_type=MESH)
+
+    def give(e, s):
+        return copy_along(sendq.at[e, s], heldq.at[e, s], q_ss.at[e, s], q_rs.at[e, s], twin)
+
+    def carry_send(e, s):
+        return copy_along(sendz.at[e, s], landz.at[1 - e, s], z_ss.at[e, s], z_rs.at[1 - e, s], at(NEAR[2 + e]))
+
+    def carry_wait(e, s):
+        return copy_along(sendz.at[e, s], landz.at[e, s], z_ss.at[e, s], z_rs.at[e, s], at(NEAR[2 + e]))
+
+    def hand(e, s):
+        return copy_along(landz.at[e, s], landq.at[e, s], h_ss.at[e, s], h_rs.at[e, s], twin)
+
+    for s in range(SPECIES):
+        for e in range(2):
+            @pl.when(inside(NEAR[2 + e]))
+            def _():
+                stage(sendq.at[e, s], safe[2 + e], s, twin_first, HALF)
+                give(e, s).start()
+
+    def straight():
+        for d in range(2):
             @pl.when(inside(NEAR[d]))
             def _():
-                for s in some:
-                    def stage(r, carry):
-                        part = pl.ds(pl.multiple_of(r * 64, 64), 64)
-                        sendp[d, s, part, :] = dense[safe[d], s, part, :]
-                        return carry
-                    lax.fori_loop(0, 4, stage, 0)
+                for s in range(SPECIES):
+                    stage(sendp.at[d, s], safe[d], s, 0, ROWS)
                     patch_send(d, s).start()
 
-    patches((0,))
 
     def face_send(d):
         return pltpu.make_async_remote_copy(
@@ -304,6 +334,13 @@
         _, rank = wanted((0, 0), step, mine)
         table[4, d:d + 1, :] = rank
     over = jnp.broadcast_to(jnp.max(jnp.max(over, axis=1, keepdims=True), axis=0, keepdims=True), (8, 128))
+    twin_base = (me + (1 - 2 * core) * ny) * CAP
+    for e, dy in enumerate((-1, 1)):
+        rel = sources((0, dy)) - me * CAP
+        other = jnp.where(core == 0, sources((1, dy)), sources((-1, dy))) - twin_base
+        both = jnp.where((rel >= 0) & (rel < CAP), 1, 0) * jnp.max(
+            jnp.where((other >= 0) & (other < CAP), 1, 0), axis=1, keepdims=True)
+        over = jnp.maximum(over, jnp.max(both, axis=1, keepdims=True))
     flags[0] = over
     to_scalars = pltpu.make_async_copy(table, table_s, tab_sem)
     to_scalars.start()
@@ -328,7 +365,17 @@
             lax.fori_loop(0, ROOM, stage, 0)
             face_send(d).start()
 
-    patches((1, 2, 3, 4))
+    straight()
+    for s in range(SPECIES):
+        for e in range(2):
+            @pl.when(inside(NEAR[2 + e]))
+            def _():
+                give(e, s).wait_recv()
+                for r in range(HALF // 64):
+                    there = pl.ds(pl.multiple_of(mine_first + r * 64, 64), 64)
+                    sendz[e, s, r * 64:r * 64 + 64, :] = jnp.where(
+                        asked[2 + e], dense[safe[2 + e], s, there, :], heldq[e, s, r * 64:r * 64 + 64, :])
+                carry_send(e, s).start()
 
     def flag_round(n, held, following):
         for k, target in enumerate(ring[n]):
@@ -397,7 +444,14 @@
         pltpu.make_async_copy(result.at[t], swept.at[t], out_sem.at[t]).start()
         return carry
 
-    lax.fori_loop(0, KEEP, stay, 0)
+    stay(0, 0)
+    for s in range(SPECIES):
+        for e in range(2):
+            @pl.when(inside(NEAR[2 + e]))
+            def _():
+                carry_wait(e, s).wait_recv()
+                hand(e, s).start()
+    stay(1, 0)
 
     flag_round(2, 2, None)
 
@@ -407,8 +461,13 @@
             face_send(d).wait_send()
             ghost_send(d).wait_send()
             for s in range(SPECIES):
-                patch_send(d, s).wait_send()
-                patch_wait(d, s).wait_recv()
+                if d < 2:
+                    patch_send(d, s).wait_send()
+                    patch_wait(d, s).wait_recv()
+                else:
+                    give(d - 2, s).wait_send()
+                    carry_send(d - 2, s).wait_send()
+                    hand(d - 2, s).wait()
             ghost_wait(d).wait_recv()
     for t in range(KEEP):
         pltpu.make_async_copy(result.at[t], swept.at[t], out_sem.at[t]).wait()
@@ -416,9 +475,9 @@
 
 def smooth_kernel(
     nx, ny,
-    src_s, mobility, fermi_gain, rates, landp, landg, swept,
+    src_s, mobility, fermi_gain, rates, landp, landz, landq, landg, swept,
     out,
-    cur, ghost, coef, base, ping, pong, blank, cur_sem, ghost_sem, out_sem, zero_sem,
+    cur, ghost, coef, base, ping, pong, blank, cur_sem, half_sem, ghost_sem, out_sem, zero_sem,
 ):
     gx, gy = lax.axis_index("gx"), lax.axis_index("gy")
     me = gx * ny + gy
@@ -436,11 +495,46 @@
     def fetch_own(t):
         return (pltpu.make_async_copy(swept.at[t], pong.at[t], cur_sem.at[t]),)
 
+    core = gx % 2
+
     def fetch_moved(t):
-        return (
-            pltpu.make_async_copy(landp.at[whence[t][3]], cur.at[t], cur_sem.at[t]),
-            pltpu.make_async_copy(landg.at[whence[t][3]], ghost.at[t], ghost_sem.at[t]),
+        came = whence[t][3]
+        e = jnp.maximum(came - 2, 0)
+        straight = (
+            pltpu.make_async_copy(landp.at[jnp.minimum(came, 1)], cur.at[t], cur_sem.at[t]),
         )
+        halves = (
+            pltpu.make_async_copy(landz.at[e], cur.at[t, :, pl.ds(pl.multiple_of(core * HALF, HALF), HALF), :], cur_sem.at[t]),
+            pltpu.make_async_copy(landq.at[e], cur.at[t, :, pl.ds(pl.multiple_of((1 - core) * HALF, HALF), HALF), :], half_sem.at[t]),
+        )
+        layers = pltpu.make_async_copy(landg.at[came], ghost.at[t], ghost_sem.at[t])
+        return straight, halves, layers
+
+    def start_moved(t):
+        straight, halves, layers = fetch_moved(t)
+        layers.start()
+
+        @pl.when(whence[t][3] < 2)
+        def _():
+            straight[0].start()
+
+        @pl.when(whence[t][3] >= 2)
+        def _():
+            halves[0].start()
+            halves[1].start()
+
+    def wait_moved(t):
+        straight, halves, layers = fetch_moved(t)
+        layers.wait()
+
+        @pl.when(whence[t][3] < 2)
+        def _():
+            straight[0].wait()
+
+        @pl.when(whence[t][3] >= 2)
+        def _():
+            halves[0].wait()
+            halves[1].wait()
 
     for t in range(KEEP):
         source, own, slot, came = whence[t]
@@ -452,8 +546,7 @@
 
         @pl.when((source >= 0) & jnp.logical_not(own))
         def _():
-            for copy in fetch_moved(t):
-                copy.start()
+            start_moved(t)
 
     blank[...] = jnp.zeros(blank.shape, jnp.float32)
     zeros = [
@@ -487,8 +580,7 @@
 
         @pl.when((source >= 0) & jnp.logical_not(own))
         def _():
-            for copy in fetch_moved(t):
-                copy.wait()
+            wait_moved(t)
             step_patch(
                 mobility, fermi_gain, rates,
                 lambda s, rows: cur[t, s, rows, :], lambda f, s, rows: ghost[t, f, s, rows, :],
@@ -520,13 +612,15 @@
     return pl.pallas_call(
         functools.partial(exchange_kernel, nx, ny),
         out_shape=(
-            jax.ShapeDtypeStruct((4, SPECIES, ROWS, 128), f32),
+            jax.ShapeDtypeStruct((2, SPECIES, ROWS, 128), f32),
+            jax.ShapeDtypeStruct((2, SPECIES, HALF, 128), f32),
+            jax.ShapeDtypeStruct((2, SPECIES, HALF, 128), f32),
             jax.ShapeDtypeStruct((4, 6, SPECIES, 8, 128), f32),
             jax.ShapeDtypeStruct((KEEP, SPECIES, ROWS, 128), f32),
             jax.ShapeDtypeStruct((8, 128), i32),
         ),
         in_specs=[anywhere()] + [in_smem()] * 5 + [in_vmem()] * 2,
-        out_specs=(anywhere(), anywhere(), anywhere(), in_vmem()),
+        out_specs=(anywhere(),) * 5 + (in_vmem(),),
         scratch_shapes=[
             pltpu.VMEM((SPECIES, CAP, B**3), f32),
             pltpu.VMEM((CAP, SPECIES, ROWS, 128), f32),
@@ -534,7 +628,10 @@
             pltpu.VMEM((13, 8, 128), i32),
             pltpu.VMEM((5, 8, 128), i32),
             pltpu.SMEM((5, 8, 128), i32),
-            pltpu.VMEM((4, SPECIES, ROWS, 128), f32),
+            pltpu.VMEM((2, SPECIES, ROWS, 128), f32),
+            pltpu.VMEM((2, SPECIES, HALF, 128), f32),
+            pltpu.VMEM((2, SPECIES, HALF, 128), f32),
+            pltpu.VMEM((2, SPECIES, HALF, 128), f32),
             pltpu.VMEM((4, ROOM, SPECIES, 8, 128), f32),
             pltpu.VMEM((4, ROOM, SPECIES, 8, 128), f32),
             pltpu.VMEM((4, 6, SPECIES, 8, 128), f32),
@@ -547,7 +644,8 @@
             dma,
             dma((12,)), dma((12,)),
             dma,
-            dma((4, SPECIES)), dma((4, SPECIES)), dma((4,)), dma((4,)), dma((4,)), dma((4,)),
+            dma((2, SPECIES)), dma((2, SPECIES)), dma((2, SPECIES)), dma((2, SPECIES)),
+            dma((2, SPECIES)), dma((2, SPECIES)), dma((2, SPECIES)), dma((2, SPECIES)), dma((4,)), dma((4,)), dma((4,)), dma((4,)),
             dma((n_flags,)), dma((n_flags,)),
             dma((KEEP,)),
         ],
@@ -555,13 +653,13 @@
     )(conc, neighbours, source, mobility, fermi_gain, rates, neighbours, source)
 
 
-def smooth(nx, ny, landp, landg, swept, source, mobility, fermi_gain, rates):
+def smooth(nx, ny, landp, landz, landq, landg, swept, source, mobility, fermi_gain, rates):
     f32 = jnp.float32
     dma = pltpu.SemaphoreType.DMA
     return pl.pallas_call(
         functools.partial(smooth_kernel, nx, ny),
         out_shape=jax.ShapeDtypeStruct((SPECIES, CAP, B**3), f32),
-        in_specs=[in_smem()] * 4 + [anywhere()] * 3,
+        in_specs=[in_smem()] * 4 + [anywhere()] * 5,
         out_specs=anywhere(),
         scratch_shapes=[
             pltpu.VMEM((KEEP, SPECIES, ROWS, 128), f32),
@@ -573,11 +671,12 @@
             pltpu.VMEM((1, CAP - KEEP, B**3), f32),
             dma((KEEP,)),
             dma((KEEP,)),
+            dma((KEEP,)),
             dma((KEEP, SPECIES)),
             dma((SPECIES,)),
         ],
         compiler_params=pltpu.CompilerParams(vmem_limit_bytes=60 * 2**20),
-    )(source, mobility, fermi_gain, rates, landp, landg, swept)
+    )(source, mobility, fermi_gain, rates, landp, landz, landq, landg, swept)
 
 
 OPPOSITE = (1, 0, 3, 2, 5, 4)
@@ -773,10 +872,10 @@
 def body(nx, ny, concentration, neighbours, source_slot, mobility, fermi_gain, rates):
     source = source_slot.reshape(1, CAP)
     conc = concentration.transpose(1, 0, 2)
-    landp, landg, swept, flag = exchange(nx, ny, conc, neighbours, source, mobility, fermi_gain, rates)
+    landp, landz, landq, landg, swept, flag = exchange(nx, ny, conc, neighbours, source, mobility, fermi_gain, rates)
 
     def common():
-        return smooth(nx, ny, landp, landg, swept, source, mobility, fermi_gain, rates).transpose(1, 0, 2)
+        return smooth(nx, ny, landp, landz, landq, landg, swept, source, mobility, fermi_gain, rates).transpose(1, 0, 2)
 
     def crowded():
         return general(concentration, neighbours, source_slot, mobility, fermi_gain, rates)

time: 47.7 us -> 48.5 us (1.017)
  the two profiles are of different devices: /device:TPU:11 before, /device:TPU:25 now
where the time goes in v2:
time: 48.5 us; the launch traced here: 48.3 us
  Pallas kernels  46.6 us (96%)
  between operations  0.86 us (2%)
  local copies, waits for them, and re-layouts  0.52 us (1%)
    pallas_call x1, Pallas kernels, exchange(): pl.pallas_call(functools.partial(exchange_kernel, nx, ny), out_shape=(jax...  39.4 us
    pallas_call x1, Pallas kernels, smooth(): pl.pallas_call(functools.partial(smooth_kernel, nx, ny), out_shape=jax.Sh...  7.2 us

profile of v2, /device:TPU:25, one launch (start us, length us, event | category | flops | bytes accessed | tf_op | source)
XLA Modules:
  0.0 48.3 jit_solution(5630562521249752528)
XLA Ops:
  0.0 0.0 copy-start.12
  0.0 0.0 copy-start.13
  0.0 39.4 %shard_map.76 = (f32[2,5,256,128]{3,2,1,0:T(8,128)}, f32[2,5,128,128]{3,2,1,0:T(8,128)}, f32[2,5,128,128]{3,2,1,0:T(8,128)}, f32[4,6,5,8,128]{4,3,2,1,0:T(8,128)...) custom-call(f32[5,6,32768]{2,1,0:T(8,128)} %bitcast.373, s32[6,6]{1,0:T(8,128)} %nbr_v.1, s32[1,6]{1,0:T(1,128)} %bitcast.382, ...), custom_call_target="tpu_custom_call" | custom-call | tf_op jit(solution)/shard_map/pallas_call | solution.py:612
  39.5 0.5 %slice.265 = s32[1,1]{1,0:T(1,128)} slice(s32[8,128]{1,0:T(8,128)S(1)} %get-tuple-element.173), slice={[0:1], [0:1]} | slice | bytes 8 | tf_op jit(solution)/shard_map/slice | solution.py:883
  40.6 0.0 copy-done.12
  40.6 0.0 copy-done.13
  40.6 7.4 %conditional.1 = (f32[6,5,32768]{2,0,1:T(8,128)}) conditional(s32[]{:T(128)} %bitcast.92, (s32[6]{0:T(128)S(1)}, f32[6,5,32768]{2,0,1:T(8,128)}, s32[6,6]{1,0:T(8,128)S(1)}, (), f32[5]{0:T(128)}, /*index=5*/f32[5]{0:T(128)}, f32[5]{0:T(128)}) %tuple.145, (s32[1,6]{1,0:T(1,128)S(1)}, f32[5]{0:T(128)}, f32[5]{0:T(128)}, f32[5]{0:T(128)}, ...), branch_computations={%region_0.17_spmd, %region_17.18_spmd} | conditional | flops 29352638 | bytes 266848192 | solution.py:883
  40.9 7.2 %branch_1_fun.1 = f32[5,6,32768]{2,1,0:T(8,128)} custom-call(s32[1,6]{1,0:T(1,128)S(1)} %get-tuple-element.158.src_s, f32[5]{0:T(128)} %get-tuple-element.159.mobility, f32[5]{0:T(128)} %get-tuple-element.160.fermi_gain, f32[5]{0:T(128)} %get-tuple-element.161.rates, f32[2,5,256,128]{3,2,1,0:T(8,128)} %get-tuple-element.162.landp, ...), custom_call_target="tpu_custom_call" | custom-call | tf_op jit(solution)/shard_map/cond/branch_1_fun/pallas_call | solution.py:659
Async XLA Ops:
  0.0 40.6 %copy-start.12 = (s32[6,6]{1,0:T(8,128)S(1)}, s32[6,6]{1,0:T(8,128)}, u32[]{:S(2)}) copy-start(s32[6,6]{1,0:T(8,128)} %nbr_v.1) | copy-start | bytes 436
  0.0 40.6 %copy-start.13 = (s32[6]{0:T(128)S(1)}, s32[6]{0:T(128)}, u32[]{:S(2)}) copy-start(s32[6]{0:T(128)} %param.15) | copy-start | bytes 76

commit v3 on v2

--- a/solution.py
+++ b/solution.py
@@ -30,19 +30,12 @@
     return lax.broadcasted_iota(jnp.int32, shape, dim)
 
 
-def step_patch(mobility, fermi_gain, rates, cell, layer, coef, base, ping, result, finish):
-    lane = iota((8, 128), 1)
-    sub = iota((8, 128), 0)
-    z = lane % 32
-    first_y = (sub == 0) & (lane < 32)
-    last_y = (sub == 7) & (lane >= 96)
-    whole = pl.ds(0, 8)
+def prepare_patch(mobility, fermi_gain, rates, cell, coef, base):
     scale = [mobility[s] / jnp.full((8, 128), 1.0 + fermi_gain[s]) for s in range(SPECIES)]
 
-    def prepare(xo, carry):
+    def planes(xo, carry):
         for xi in range(8):
-            x = xo * 8 + xi
-            plane = pl.ds(pl.multiple_of(x * 8, 8), 8)
+            plane = pl.ds(pl.multiple_of(xo * 64 + xi * 8, 8), 8)
             a, i, v, p, q = [cell(s, plane) for s in range(SPECIES)]
             half = 0.5 * (a + p + q)
             electrons = half + jnp.sqrt(half * half + 1.0)
@@ -53,24 +46,38 @@
             for s in range(SPECIES):
                 spread = scale[s] * (1.0 + fermi_gain[s] * electrons)
                 inverse = 1.0 / (1.0 + 6.0 * spread)
-                low = pltpu.roll(layer(4, s, whole), (128 - x) % 128, 1)
-                high = pltpu.roll(layer(5, s, whole), (31 - x + 128) % 128, 1)
-                extra = jnp.where(z == 0, low, jnp.where(z == 31, high, 0.0))
-                low = jnp.broadcast_to(layer(2, s, pl.ds(xi, 1)), (8, 128))
-                high = jnp.broadcast_to(layer(3, s, pl.ds(xi, 1)), (8, 128))
-                low = pltpu.roll(low, (128 - 32 * xo) % 128, 1)
-                high = pltpu.roll(high, (96 - 32 * xo) % 128, 1)
-                extra = extra + jnp.where(first_y, low, jnp.where(last_y, high, 0.0))
-                if xi == 0:
-                    extra = extra + jnp.where(x == 0, layer(0, s, whole), 0.0)
-                if xi == 7:
-                    extra = extra + jnp.where(x == B - 1, layer(1, s, whole), 0.0)
-                weight = spread * inverse
-                coef[s, plane, :] = weight
-                base[s, plane, :] = sources[s] * inverse + weight * extra
+                coef[s, plane, :] = spread * inverse
+                base[s, plane, :] = sources[s] * inverse
         return carry
 
-    lax.fori_loop(0, 4, prepare, 0)
+    lax.fori_loop(0, 4, planes, 0)
+
+
+def sweep_patch(cell, layer, coef, base, ping, result, finish):
+    lane = iota((8, 128), 1)
+    sub = iota((8, 128), 0)
+    z = lane % 32
+    first_y = (sub == 0) & (lane < 32)
+    last_y = (sub == 7) & (lane >= 96)
+    whole = pl.ds(0, 8)
+
+    def ghosts(s):
+        for x in range(B):
+            plane = pl.ds(8 * x, 8)
+            low = pltpu.roll(layer(4, s, whole), (128 - x) % 128, 1) if x else layer(4, s, whole)
+            high = pltpu.roll(layer(5, s, whole), 31 - x, 1) if x < 31 else layer(5, s, whole)
+            extra = jnp.where(z == 0, low, jnp.where(z == 31, high, 0.0))
+            low = jnp.broadcast_to(layer(2, s, pl.ds(x % 8, 1)), (8, 128))
+            high = jnp.broadcast_to(layer(3, s, pl.ds(x % 8, 1)), (8, 128))
+            xo = x // 8
+            low = pltpu.roll(low, 128 - 32 * xo, 1) if xo else low
+            high = pltpu.roll(high, 96 - 32 * xo, 1) if xo < 3 else high
+            extra = extra + jnp.where(first_y, low, jnp.where(last_y, high, 0.0))
+            if x == 0:
+                extra = extra + layer(0, s, whole)
+            if x == B - 1:
+                extra = extra + layer(1, s, whole)
+            base[s, plane, :] = base[s, plane, :] + coef[s, plane, :] * extra
 
     def species(s, carry):
         def sweep(get, put):
@@ -97,6 +104,7 @@
         def put_result(x, value):
             result[s, 8 * x:8 * x + 8, :] = value
 
+        ghosts(s)
         sweep(lambda x: cell(s, pl.ds(8 * x, 8)), put_result)
         sweep(lambda x: result[s, 8 * x:8 * x + 8, :], put_ping)
         sweep(lambda x: ping[8 * x:8 * x + 8, :], put_result)
@@ -236,12 +244,6 @@
             src_ref=sendp.at[d, s], dst_ref=landp.at[d, s], send_sem=p_ss.at[d, s], recv_sem=p_rs.at[d, s],
             device_id=at(NEAR[d]), device_id_type=MESH)
 
-    def stage(to, slot, s, first, rows):
-        def part(r, carry):
-            to[pl.ds(pl.multiple_of(r * 64, 64), 64), :] = dense[slot, s, pl.ds(pl.multiple_of(first + r * 64, 64), 64), :]
-            return carry
-        lax.fori_loop(0, rows // 64, part, 0)
-
     core = gx % 2
     twin = (gx + 1 - 2 * core, gy)
     mine_first, twin_first = core * HALF, (1 - core) * HALF
@@ -266,7 +268,7 @@
         for e in range(2):
             @pl.when(inside(NEAR[2 + e]))
             def _():
-                stage(sendq.at[e, s], safe[2 + e], s, twin_first, HALF)
+                sendq[e, s] = dense[safe[2 + e], s, pl.ds(pl.multiple_of(twin_first, HALF), HALF), :]
                 give(e, s).start()
 
     def straight():
@@ -274,7 +276,7 @@
             @pl.when(inside(NEAR[d]))
             def _():
                 for s in range(SPECIES):
-                    stage(sendp.at[d, s], safe[d], s, 0, ROWS)
+                    sendp[d, s] = dense[safe[d], s]
                     patch_send(d, s).start()
 
 
@@ -371,10 +373,8 @@
             @pl.when(inside(NEAR[2 + e]))
             def _():
                 give(e, s).wait_recv()
-                for r in range(HALF // 64):
-                    there = pl.ds(pl.multiple_of(mine_first + r * 64, 64), 64)
-                    sendz[e, s, r * 64:r * 64 + 64, :] = jnp.where(
-                        asked[2 + e], dense[safe[2 + e], s, there, :], heldq[e, s, r * 64:r * 64 + 64, :])
+                own = dense[safe[2 + e], s, pl.ds(pl.multiple_of(mine_first, HALF), HALF), :]
+                sendz[e, s] = jnp.where(asked[2 + e], own, heldq[e, s])
                 carry_send(e, s).start()
 
     def flag_round(n, held, following):
@@ -391,7 +391,17 @@
             for k, target in enumerate(ring[n + 1]):
                 flag_copy(bases[n + 1], k, target, following).start()
 
-    flag_round(0, 0, 1)
+    kept = []
+    for t in range(KEEP):
+        rel = src_s[0, t] - me * CAP
+        kept.append(jnp.where((rel >= 0) & (rel < CAP), rel, 0))
+
+    def ready(t, carry):
+        slot = jnp.where(t == 0, kept[0], kept[1])
+        prepare_patch(
+            mobility, fermi_gain, rates, lambda s, rows: dense[slot, s, rows, :], coef.at[t], base.at[t])
+        return carry
+    lax.fori_loop(0, KEEP, ready, 0)
 
     for d, step in enumerate(NEAR):
         @pl.when(inside(step))
@@ -427,31 +437,29 @@
             lax.fori_loop(0, 6, stage, 0)
             ghost_send(d).start()
 
-    flag_round(1, 1, 2)
-
-    def stay(t, carry):
-        rel = src_s[0, t] - me * CAP
-        slot = jnp.where((rel >= 0) & (rel < CAP), rel, 0)
+    flag_round(0, 0, 1)
+
+    def stay(t):
+        slot = kept[t]
 
         def layer(f, carry):
             ghost[f] = ghost_value(slot, f)
             return carry
         lax.fori_loop(0, 6, layer, 0)
-        step_patch(
-            mobility, fermi_gain, rates,
+        sweep_patch(
             lambda s, rows: dense[slot, s, rows, :], lambda f, s, rows: ghost[f, s, rows, :],
-            coef, base, ping, result.at[t], lambda s: None)
+            coef.at[t], base.at[t], ping, result.at[t], lambda s: None)
         pltpu.make_async_copy(result.at[t], swept.at[t], out_sem.at[t]).start()
-        return carry
-
-    stay(0, 0)
+
+    stay(0)
+    flag_round(1, 1, 2)
     for s in range(SPECIES):
         for e in range(2):
             @pl.when(inside(NEAR[2 + e]))
             def _():
                 carry_wait(e, s).wait_recv()
                 hand(e, s).start()
-    stay(1, 0)
+    stay(1)
 
     flag_round(2, 2, None)
 
@@ -581,10 +589,10 @@
         @pl.when((source >= 0) & jnp.logical_not(own))
         def _():
             wait_moved(t)
-            step_patch(
-                mobility, fermi_gain, rates,
-                lambda s, rows: cur[t, s, rows, :], lambda f, s, rows: ghost[t, f, s, rows, :],
-                coef, base, ping, pong.at[t], lambda s: put_out(t, s).start())
+            prepare_patch(mobility, fermi_gain, rates, lambda s, rows: cur[t, s, rows, :], coef, base)
+            sweep_patch(
+                lambda s, rows: cur[t, s, rows, :], lambda f, s, rows: ghost[t, f, s, rows, :], coef, base, ping, pong.at[t],
+                lambda s: put_out(t, s).start())
 
     for copy in zeros:
         copy.wait()
@@ -637,8 +645,8 @@
             pltpu.VMEM((4, 6, SPECIES, 8, 128), f32),
             pltpu.VMEM((n_flags, 8, 128), i32),
             pltpu.VMEM((6, SPECIES, 8, 128), f32),
-            pltpu.VMEM((SPECIES, ROWS, 128), f32),
-            pltpu.VMEM((SPECIES, ROWS, 128), f32),
+            pltpu.VMEM((KEEP, SPECIES, ROWS, 128), f32),
+            pltpu.VMEM((KEEP, SPECIES, ROWS, 128), f32),
             pltpu.VMEM((ROWS, 128), f32),
             pltpu.VMEM((KEEP, SPECIES, ROWS, 128), f32),
             dma,

time: 48.5 us -> 46.4 us (0.957)
  the two profiles are of different devices: /device:TPU:25 before, /device:TPU:1 now
where the time goes in v3:
time: 46.4 us; the launch traced here: 46.1 us
  Pallas kernels  44.5 us (96%)
  between operations  0.86 us (2%)
  local copies, waits for them, and re-layouts  0.52 us (1%)
    pallas_call x1, Pallas kernels, exchange(): pl.pallas_call(functools.partial(exchange_kernel, nx, ny), out_shape=(jax...  37.3 us
    pallas_call x1, Pallas kernels, smooth(): pl.pallas_call(functools.partial(smooth_kernel, nx, ny), out_shape=jax.Sh...  7.19 us

profile of v3, /device:TPU:1, one launch (start us, length us, event | category | flops | bytes accessed | tf_op | source)
XLA Modules:
  0.0 46.1 jit_solution(17947165982269193311)
XLA Ops:
  0.0 0.0 copy-start.12
  0.0 0.0 copy-start.13
  0.0 37.3 %shard_map.76 = (f32[2,5,256,128]{3,2,1,0:T(8,128)}, f32[2,5,128,128]{3,2,1,0:T(8,128)}, f32[2,5,128,128]{3,2,1,0:T(8,128)}, f32[4,6,5,8,128]{4,3,2,1,0:T(8,128)...) custom-call(f32[5,6,32768]{2,1,0:T(8,128)} %bitcast.373, s32[6,6]{1,0:T(8,128)} %nbr_v.1, s32[1,6]{1,0:T(1,128)} %bitcast.382, ...), custom_call_target="tpu_custom_call" | custom-call | tf_op jit(solution)/shard_map/pallas_call | solution.py:620
  37.3 0.5 %slice.265 = s32[1,1]{1,0:T(1,128)} slice(s32[8,128]{1,0:T(8,128)S(1)} %get-tuple-element.173), slice={[0:1], [0:1]} | slice | bytes 8 | tf_op jit(solution)/shard_map/slice | solution.py:891
  38.5 0.0 copy-done.12
  38.5 0.0 copy-done.13
  38.5 7.4 %conditional.1 = (f32[6,5,32768]{2,0,1:T(8,128)}) conditional(s32[]{:T(128)} %bitcast.92, (s32[6]{0:T(128)S(1)}, f32[6,5,32768]{2,0,1:T(8,128)}, s32[6,6]{1,0:T(8,128)S(1)}, (), f32[5]{0:T(128)}, /*index=5*/f32[5]{0:T(128)}, f32[5]{0:T(128)}) %tuple.145, (s32[1,6]{1,0:T(1,128)S(1)}, f32[5]{0:T(128)}, f32[5]{0:T(128)}, f32[5]{0:T(128)}, ...), branch_computations={%region_0.17_spmd, %region_17.18_spmd} | conditional | flops 29352638 | bytes 266848192 | solution.py:891
  38.7 7.2 %branch_1_fun.1 = f32[5,6,32768]{2,1,0:T(8,128)} custom-call(s32[1,6]{1,0:T(1,128)S(1)} %get-tuple-element.158.src_s, f32[5]{0:T(128)} %get-tuple-element.159.mobility, f32[5]{0:T(128)} %get-tuple-element.160.fermi_gain, f32[5]{0:T(128)} %get-tuple-element.161.rates, f32[2,5,256,128]{3,2,1,0:T(8,128)} %get-tuple-element.162.landp, ...), custom_call_target="tpu_custom_call" | custom-call | tf_op jit(solution)/shard_map/cond/branch_1_fun/pallas_call | solution.py:667
Async XLA Ops:
  0.0 38.5 %copy-start.12 = (s32[6,6]{1,0:T(8,128)S(1)}, s32[6,6]{1,0:T(8,128)}, u32[]{:S(2)}) copy-start(s32[6,6]{1,0:T(8,128)} %nbr_v.1) | copy-start | bytes 436
  0.0 38.5 %copy-start.13 = (s32[6]{0:T(128)S(1)}, s32[6]{0:T(128)}, u32[]{:S(2)}) copy-start(s32[6]{0:T(128)} %param.15) | copy-start | bytes 76

commit v4 on v3

--- a/solution.py
+++ b/solution.py
@@ -38,14 +38,17 @@
             plane = pl.ds(pl.multiple_of(xo * 64 + xi * 8, 8), 8)
             a, i, v, p, q = [cell(s, plane) for s in range(SPECIES)]
             half = 0.5 * (a + p + q)
-            electrons = half + jnp.sqrt(half * half + 1.0)
+            square = half * half + 1.0
+            electrons = half + square * lax.rsqrt(square)
             ai = rates[0] * a * i - rates[1] * p
             av = rates[2] * a * v - rates[3] * q
             re = rates[4] * (i * v - 1.0)
             sources = (a - ai - av, i - ai - re, v - av - re, p + ai, q + av)
             for s in range(SPECIES):
                 spread = scale[s] * (1.0 + fermi_gain[s] * electrons)
-                inverse = 1.0 / (1.0 + 6.0 * spread)
+                diagonal = 1.0 + 6.0 * spread
+                inverse = pl.reciprocal(diagonal, approx=True)
+                inverse = inverse * (2.0 - diagonal * inverse)
                 coef[s, plane, :] = spread * inverse
                 base[s, plane, :] = sources[s] * inverse
         return carry
@@ -367,16 +370,6 @@
             lax.fori_loop(0, ROOM, stage, 0)
             face_send(d).start()
 
-    straight()
-    for s in range(SPECIES):
-        for e in range(2):
-            @pl.when(inside(NEAR[2 + e]))
-            def _():
-                give(e, s).wait_recv()
-                own = dense[safe[2 + e], s, pl.ds(pl.multiple_of(mine_first, HALF), HALF), :]
-                sendz[e, s] = jnp.where(asked[2 + e], own, heldq[e, s])
-                carry_send(e, s).start()
-
     def flag_round(n, held, following):
         for k, target in enumerate(ring[n]):
             copy = flag_copy(bases[n], k, target, held)
@@ -396,12 +389,22 @@
         rel = src_s[0, t] - me * CAP
         kept.append(jnp.where((rel >= 0) & (rel < CAP), rel, 0))
 
-    def ready(t, carry):
-        slot = jnp.where(t == 0, kept[0], kept[1])
+    def ready(t):
+        slot = kept[t]
         prepare_patch(
             mobility, fermi_gain, rates, lambda s, rows: dense[slot, s, rows, :], coef.at[t], base.at[t])
-        return carry
-    lax.fori_loop(0, KEEP, ready, 0)
+    ready(0)
+    for s in range(SPECIES):
+        for e in range(2):
+            @pl.when(inside(NEAR[2 + e]))
+            def _():
+                give(e, s).wait_recv()
+                own = dense[safe[2 + e], s, pl.ds(pl.multiple_of(mine_first, HALF), HALF), :]
+                sendz[e, s] = jnp.where(asked[2 + e], own, heldq[e, s])
+                carry_send(e, s).start()
+    flag_round(0, 0, 1)
+    straight()
+    ready(1)
 
     for d, step in enumerate(NEAR):
         @pl.when(inside(step))
@@ -437,7 +440,7 @@
             lax.fori_loop(0, 6, stage, 0)
             ghost_send(d).start()
 
-    flag_round(0, 0, 1)
+    flag_round(1, 1, 2)
 
     def stay(t):
         slot = kept[t]
@@ -452,16 +455,14 @@
         pltpu.make_async_copy(result.at[t], swept.at[t], out_sem.at[t]).start()
 
     stay(0)
-    flag_round(1, 1, 2)
+    flag_round(2, 2, None)
+    stay(1)
     for s in range(SPECIES):
         for e in range(2):
             @pl.when(inside(NEAR[2 + e]))
             def _():
                 carry_wait(e, s).wait_recv()
                 hand(e, s).start()
-    stay(1)
-
-    flag_round(2, 2, None)
 
     for d, step in enumerate(NEAR):
         @pl.when(inside(step))

time: 46.4 us -> 48.4 us (1.043)
  the two profiles are of different devices: /device:TPU:1 before, /device:TPU:11 now
where the time goes in v4:
time: 48.4 us; the launch traced here: 48.1 us
  Pallas kernels  46.5 us (96%)
  between operations  0.86 us (2%)
  local copies, waits for them, and re-layouts  0.52 us (1%)
    pallas_call x1, Pallas kernels, exchange(): pl.pallas_call(functools.partial(exchange_kernel, nx, ny), out_shape=(jax...  39.2 us
    pallas_call x1, Pallas kernels, smooth(): pl.pallas_call(functools.partial(smooth_kernel, nx, ny), out_shape=jax.Sh...  7.22 us

profile of v4, /device:TPU:11, one launch (start us, length us, event | category | flops | bytes accessed | tf_op | source)
XLA Modules:
  0.0 48.1 jit_solution(2729205024695897243)
XLA Ops:
  0.0 0.0 copy-start.12
  0.0 0.0 copy-start.13
  0.0 39.2 %shard_map.76 = (f32[2,5,256,128]{3,2,1,0:T(8,128)}, f32[2,5,128,128]{3,2,1,0:T(8,128)}, f32[2,5,128,128]{3,2,1,0:T(8,128)}, f32[4,6,5,8,128]{4,3,2,1,0:T(8,128)...) custom-call(f32[5,6,32768]{2,1,0:T(8,128)} %bitcast.373, s32[6,6]{1,0:T(8,128)} %nbr_v.1, s32[1,6]{1,0:T(1,128)} %bitcast.382, ...), custom_call_target="tpu_custom_call" | custom-call | tf_op jit(solution)/shard_map/pallas_call | solution.py:621
  39.3 0.5 %slice.265 = s32[1,1]{1,0:T(1,128)} slice(s32[8,128]{1,0:T(8,128)S(1)} %get-tuple-element.173), slice={[0:1], [0:1]} | slice | bytes 8 | tf_op jit(solution)/shard_map/slice | solution.py:892
  40.4 0.0 copy-done.12
  40.4 0.0 copy-done.13
  40.4 7.5 %conditional.1 = (f32[6,5,32768]{2,0,1:T(8,128)}) conditional(s32[]{:T(128)} %bitcast.92, (s32[6]{0:T(128)S(1)}, f32[6,5,32768]{2,0,1:T(8,128)}, s32[6,6]{1,0:T(8,128)S(1)}, (), f32[5]{0:T(128)}, /*index=5*/f32[5]{0:T(128)}, f32[5]{0:T(128)}) %tuple.145, (s32[1,6]{1,0:T(1,128)S(1)}, f32[5]{0:T(128)}, f32[5]{0:T(128)}, f32[5]{0:T(128)}, ...), branch_computations={%region_0.17_spmd, %region_17.18_spmd} | conditional | flops 29352638 | bytes 266848192 | solution.py:892
  40.7 7.2 %branch_1_fun.1 = f32[5,6,32768]{2,1,0:T(8,128)} custom-call(s32[1,6]{1,0:T(1,128)S(1)} %get-tuple-element.158.src_s, f32[5]{0:T(128)} %get-tuple-element.159.mobility, f32[5]{0:T(128)} %get-tuple-element.160.fermi_gain, f32[5]{0:T(128)} %get-tuple-element.161.rates, f32[2,5,256,128]{3,2,1,0:T(8,128)} %get-tuple-element.162.landp, ...), custom_call_target="tpu_custom_call" | custom-call | tf_op jit(solution)/shard_map/cond/branch_1_fun/pallas_call | solution.py:668
Async XLA Ops:
  0.0 40.4 %copy-start.12 = (s32[6,6]{1,0:T(8,128)S(1)}, s32[6,6]{1,0:T(8,128)}, u32[]{:S(2)}) copy-start(s32[6,6]{1,0:T(8,128)} %nbr_v.1) | copy-start | bytes 436
  0.0 40.4 %copy-start.13 = (s32[6]{0:T(128)S(1)}, s32[6]{0:T(128)}, u32[]{:S(2)}) copy-start(s32[6]{0:T(128)} %param.15) | copy-start | bytes 76

commit v5 on v3

--- a/solution.py
+++ b/solution.py
@@ -38,14 +38,17 @@
             plane = pl.ds(pl.multiple_of(xo * 64 + xi * 8, 8), 8)
             a, i, v, p, q = [cell(s, plane) for s in range(SPECIES)]
             half = 0.5 * (a + p + q)
-            electrons = half + jnp.sqrt(half * half + 1.0)
+            square = half * half + 1.0
+            electrons = half + square * lax.rsqrt(square)
             ai = rates[0] * a * i - rates[1] * p
             av = rates[2] * a * v - rates[3] * q
             re = rates[4] * (i * v - 1.0)
             sources = (a - ai - av, i - ai - re, v - av - re, p + ai, q + av)
             for s in range(SPECIES):
                 spread = scale[s] * (1.0 + fermi_gain[s] * electrons)
-                inverse = 1.0 / (1.0 + 6.0 * spread)
+                diagonal = 1.0 + 6.0 * spread
+                inverse = pl.reciprocal(diagonal, approx=True)
+                inverse = inverse * (2.0 - diagonal * inverse)
                 coef[s, plane, :] = spread * inverse
                 base[s, plane, :] = sources[s] * inverse
         return carry
@@ -137,8 +140,8 @@
     row, col = gy // 4, gy % 4
     ring = (
         [(gx, row * 4 + (col + k) % 4) for k in range(1, 4)],
+        [(gx, ((row + k) % 4) * 4 + col) for k in range(1, 4)],
         [((gx + k) % nx, gy) for k in range(1, nx)],
-        [(gx, ((row + k) % 4) * 4 + col) for k in range(1, 4)],
     )
 
     meta[...] = jnp.full(meta.shape, -1, jnp.int32)
@@ -352,7 +355,7 @@
             src_ref=flags.at[held], dst_ref=flags.at[base + k], send_sem=fl_ss.at[base + k],
             recv_sem=fl_rs.at[base + k], device_id=target, device_id_type=MESH)
 
-    bases = (3, 6, 6 + nx - 1)
+    bases = (3, 6, 9)
 
     for k, target in enumerate(ring[0]):
         flag_copy(bases[0], k, target, 0).start()
@@ -401,6 +404,7 @@
         prepare_patch(
             mobility, fermi_gain, rates, lambda s, rows: dense[slot, s, rows, :], coef.at[t], base.at[t])
         return carry
+    flag_round(0, 0, 1)
     lax.fori_loop(0, KEEP, ready, 0)
 
     for d, step in enumerate(NEAR):
@@ -437,7 +441,7 @@
             lax.fori_loop(0, 6, stage, 0)
             ghost_send(d).start()
 
-    flag_round(0, 0, 1)
+    flag_round(1, 1, 2)
 
     def stay(t):
         slot = kept[t]
@@ -452,7 +456,6 @@
         pltpu.make_async_copy(result.at[t], swept.at[t], out_sem.at[t]).start()
 
     stay(0)
-    flag_round(1, 1, 2)
     for s in range(SPECIES):
         for e in range(2):
             @pl.when(inside(NEAR[2 + e]))

time: 46.4 us -> 48 us (1.034)
  the two profiles are of different devices: /device:TPU:1 before, /device:TPU:11 now
where the time goes in v5:
time: 48 us; the launch traced here: 47.8 us
  Pallas kernels  46.2 us (96%)
  between operations  0.86 us (2%)
  local copies, waits for them, and re-layouts  0.52 us (1%)
    pallas_call x1, Pallas kernels, exchange(): pl.pallas_call(functools.partial(exchange_kernel, nx, ny), out_shape=(jax...  38.9 us
    pallas_call x1, Pallas kernels, smooth(): pl.pallas_call(functools.partial(smooth_kernel, nx, ny), out_shape=jax.Sh...  7.22 us

profile of v5, /device:TPU:11, one launch (start us, length us, event | category | flops | bytes accessed | tf_op | source)
XLA Modules:
  0.0 47.8 jit_solution(3760906858346726952)
XLA Ops:
  0.0 0.0 copy-start.12
  0.0 0.0 copy-start.13
  0.0 38.9 %shard_map.76 = (f32[2,5,256,128]{3,2,1,0:T(8,128)}, f32[2,5,128,128]{3,2,1,0:T(8,128)}, f32[2,5,128,128]{3,2,1,0:T(8,128)}, f32[4,6,5,8,128]{4,3,2,1,0:T(8,128)...) custom-call(f32[5,6,32768]{2,1,0:T(8,128)} %bitcast.373, s32[6,6]{1,0:T(8,128)} %nbr_v.1, s32[1,6]{1,0:T(1,128)} %bitcast.382, ...), custom_call_target="tpu_custom_call" | custom-call | tf_op jit(solution)/shard_map/pallas_call | solution.py:623
  38.9 0.5 %slice.265 = s32[1,1]{1,0:T(1,128)} slice(s32[8,128]{1,0:T(8,128)S(1)} %get-tuple-element.173), slice={[0:1], [0:1]} | slice | bytes 8 | tf_op jit(solution)/shard_map/slice | solution.py:894
  40.1 0.0 copy-done.12
  40.1 0.0 copy-done.13
  40.1 7.5 %conditional.1 = (f32[6,5,32768]{2,0,1:T(8,128)}) conditional(s32[]{:T(128)} %bitcast.92, (s32[6]{0:T(128)S(1)}, f32[6,5,32768]{2,0,1:T(8,128)}, s32[6,6]{1,0:T(8,128)S(1)}, (), f32[5]{0:T(128)}, /*index=5*/f32[5]{0:T(128)}, f32[5]{0:T(128)}) %tuple.145, (s32[1,6]{1,0:T(1,128)S(1)}, f32[5]{0:T(128)}, f32[5]{0:T(128)}, f32[5]{0:T(128)}, ...), branch_computations={%region_0.17_spmd, %region_17.18_spmd} | conditional | flops 29352638 | bytes 266848192 | solution.py:894
  40.4 7.2 %branch_1_fun.1 = f32[5,6,32768]{2,1,0:T(8,128)} custom-call(s32[1,6]{1,0:T(1,128)S(1)} %get-tuple-element.158.src_s, f32[5]{0:T(128)} %get-tuple-element.159.mobility, f32[5]{0:T(128)} %get-tuple-element.160.fermi_gain, f32[5]{0:T(128)} %get-tuple-element.161.rates, f32[2,5,256,128]{3,2,1,0:T(8,128)} %get-tuple-element.162.landp, ...), custom_call_target="tpu_custom_call" | custom-call | tf_op jit(solution)/shard_map/cond/branch_1_fun/pallas_call | solution.py:670
Async XLA Ops:
  0.0 40.1 %copy-start.12 = (s32[6,6]{1,0:T(8,128)S(1)}, s32[6,6]{1,0:T(8,128)}, u32[]{:S(2)}) copy-start(s32[6,6]{1,0:T(8,128)} %nbr_v.1) | copy-start | bytes 436
  0.0 40.1 %copy-start.13 = (s32[6]{0:T(128)S(1)}, s32[6]{0:T(128)}, u32[]{:S(2)}) copy-start(s32[6]{0:T(128)} %param.15) | copy-start | bytes 76

commit v6 on v3

--- a/solution.py
+++ b/solution.py
@@ -137,8 +137,8 @@
     row, col = gy // 4, gy % 4
     ring = (
         [(gx, row * 4 + (col + k) % 4) for k in range(1, 4)],
+        [(gx, ((row + k) % 4) * 4 + col) for k in range(1, 4)],
         [((gx + k) % nx, gy) for k in range(1, nx)],
-        [(gx, ((row + k) % 4) * 4 + col) for k in range(1, 4)],
     )
 
     meta[...] = jnp.full(meta.shape, -1, jnp.int32)
@@ -352,7 +352,7 @@
             src_ref=flags.at[held], dst_ref=flags.at[base + k], send_sem=fl_ss.at[base + k],
             recv_sem=fl_rs.at[base + k], device_id=target, device_id_type=MESH)
 
-    bases = (3, 6, 6 + nx - 1)
+    bases = (3, 6, 9)
 
     for k, target in enumerate(ring[0]):
         flag_copy(bases[0], k, target, 0).start()
@@ -407,6 +407,8 @@
         @pl.when(inside(step))
         def _():
             face_wait(d).wait_recv()
+
+    flag_round(0, 0, 1)
 
     def ghost_place(slot, f):
         nb = nbr_s[slot, f]
@@ -436,8 +438,6 @@
                 return carry
             lax.fori_loop(0, 6, stage, 0)
             ghost_send(d).start()
-
-    flag_round(0, 0, 1)
 
     def stay(t):
         slot = kept[t]

time: 46.4 us -> 45 us (0.970)
  the two profiles are of different devices: /device:TPU:1 before, /device:TPU:11 now
where the time goes in v6:
time: 45 us; the launch traced here: 44.5 us
  Pallas kernels  42.9 us (95%)
  between operations  0.86 us (2%)
  local copies, waits for them, and re-layouts  0.52 us (1%)
    pallas_call x1, Pallas kernels, exchange(): pl.pallas_call(functools.partial(exchange_kernel, nx, ny), out_shape=(jax...  35.7 us
    pallas_call x1, Pallas kernels, smooth(): pl.pallas_call(functools.partial(smooth_kernel, nx, ny), out_shape=jax.Sh...  7.2 us

profile of v6, /device:TPU:11, one launch (start us, length us, event | category | flops | bytes accessed | tf_op | source)
XLA Modules:
  0.0 44.5 jit_solution(3335138607098981553)
XLA Ops:
  0.0 0.0 copy-start.12
  0.0 0.0 copy-start.13
  0.0 35.7 %shard_map.76 = (f32[2,5,256,128]{3,2,1,0:T(8,128)}, f32[2,5,128,128]{3,2,1,0:T(8,128)}, f32[2,5,128,128]{3,2,1,0:T(8,128)}, f32[4,6,5,8,128]{4,3,2,1,0:T(8,128)...) custom-call(f32[5,6,32768]{2,1,0:T(8,128)} %bitcast.373, s32[6,6]{1,0:T(8,128)} %nbr_v.1, s32[1,6]{1,0:T(1,128)} %bitcast.382, ...), custom_call_target="tpu_custom_call" | custom-call | tf_op jit(solution)/shard_map/pallas_call | solution.py:620
  35.7 0.5 %slice.265 = s32[1,1]{1,0:T(1,128)} slice(s32[8,128]{1,0:T(8,128)S(1)} %get-tuple-element.173), slice={[0:1], [0:1]} | slice | bytes 8 | tf_op jit(solution)/shard_map/slice | solution.py:891
  36.9 0.0 copy-done.12
  36.9 0.0 copy-done.13
  36.9 7.4 %conditional.1 = (f32[6,5,32768]{2,0,1:T(8,128)}) conditional(s32[]{:T(128)} %bitcast.92, (s32[6]{0:T(128)S(1)}, f32[6,5,32768]{2,0,1:T(8,128)}, s32[6,6]{1,0:T(8,128)S(1)}, (), f32[5]{0:T(128)}, /*index=5*/f32[5]{0:T(128)}, f32[5]{0:T(128)}) %tuple.145, (s32[1,6]{1,0:T(1,128)S(1)}, f32[5]{0:T(128)}, f32[5]{0:T(128)}, f32[5]{0:T(128)}, ...), branch_computations={%region_0.17_spmd, %region_17.18_spmd} | conditional | flops 29352638 | bytes 266848192 | solution.py:891
  37.1 7.2 %branch_1_fun.1 = f32[5,6,32768]{2,1,0:T(8,128)} custom-call(s32[1,6]{1,0:T(1,128)S(1)} %get-tuple-element.158.src_s, f32[5]{0:T(128)} %get-tuple-element.159.mobility, f32[5]{0:T(128)} %get-tuple-element.160.fermi_gain, f32[5]{0:T(128)} %get-tuple-element.161.rates, f32[2,5,256,128]{3,2,1,0:T(8,128)} %get-tuple-element.162.landp, ...), custom_call_target="tpu_custom_call" | custom-call | tf_op jit(solution)/shard_map/cond/branch_1_fun/pallas_call | solution.py:667
Async XLA Ops:
  0.0 36.9 %copy-start.12 = (s32[6,6]{1,0:T(8,128)S(1)}, s32[6,6]{1,0:T(8,128)}, u32[]{:S(2)}) copy-start(s32[6,6]{1,0:T(8,128)} %nbr_v.1) | copy-start | bytes 436
  0.0 36.9 %copy-start.13 = (s32[6]{0:T(128)S(1)}, s32[6]{0:T(128)}, u32[]{:S(2)}) copy-start(s32[6]{0:T(128)} %param.15) | copy-start | bytes 76
